TPU v7x, 32 devices: a whole 2x2x4 slice. The times are simulated.
32 devices in a mesh: lat: 8 (over z, core), lon: 4 (over y, x).
Axes of the slice: x: 2, y: 2, z: 4, core: 2. Of those that a mesh axis runs over, the one named last changes fastest.
Arguments:
- tokens: bfloat16 [4, 48, 96, 192], P(None, 'lat', 'lon'), may hold values from -6 to 6
- cotangent: bfloat16 [4, 48, 96, 192], P(None, 'lat', 'lon'), may hold values from -6 to 6
- norm_gain: float32 [192], replicated, may hold values from 0.1 to 1.9
- inproj_weight: bfloat16 [192, 576], replicated, may hold values from -0.4375 to 0.4375
- outproj_weight: bfloat16 [192, 192], replicated, may hold values from -0.4375 to 0.4375
- bias: float32 [2, 8, 6, 144, 144], P(None, 'lat'), may hold values from -4 to 4
Outputs:
- grad_input: bfloat16 [4, 48, 96, 192], P(None, 'lat', 'lon')
- bias_grad: float32 [2, 8, 6, 144, 144], P(None, 'lat', None, 'lon')
All inputs are finite; a program needn't handle non-finite values.
Results may differ from a plain program's by a relative error of at most 0.017.
Values may be sent and summed in bfloat16 or wider, within the bound.
No kernel may reach another device: no remote copies, remote signals or barrier semaphores. Data moves between devices by JAX's collectives and lax.ppermute only.
A program may use at most 64 MiB of HBM per device.

v0:
```python
import functools

import jax
import jax.numpy as jnp
import numpy as np
from jax import lax
from jax.experimental import pallas as pl
from jax.experimental.pallas import tpu as pltpu
from jax.sharding import PartitionSpec as P

WZ = 2
WH = 6
WW = 12
WT = WZ * WH * WW
HALF_ROWS = WH // 2
HALF_COLS = WW // 2
SIDE = 8
LEVEL = WH * WW
LANES = 128
LOG2E = 1.4426950408889634
epsilon = 1e-05
F32 = jnp.float32
BF16 = jnp.bfloat16
NT = (((1,), (1,)), ((), ()))


def dot(a, b):
    return jnp.dot(a, b, preferred_element_type=F32)


def dot_nt(a, b):
    return lax.dot_general(a, b, NT, preferred_element_type=F32)


def round_up(value, to):
    return (value + to - 1) // to * to


class Chunks:
    def __init__(self, parts, heads):
        self.parts, self.heads = parts, heads
        self.size = WT // parts
        self.main = self.size // 16 * 16
        self.rest = self.size - self.main
        self.rest_rows = round_up(heads * self.rest, 16)
        self.rows = self.main + self.rest_rows
        self.used = heads * self.main + self.rest_rows
        self.width = round_up(self.used, LANES)

    def queries(self):
        table = np.zeros((self.parts, self.rows, WT), np.float32)
        for j in range(self.parts):
            for i in range(self.main):
                table[j, i, j * self.size + i] = 1.0
            for h in range(self.heads):
                for i in range(self.rest):
                    table[j, self.main + h * self.rest + i, j * self.size + self.main + i] = 1.0
        return table

    def columns(self, j):
        lane = lax.broadcasted_iota(jnp.int32, (1, self.width), 1)
        low = self.heads * self.main
        main, left = lane, self.main + lane - low
        for h in range(1, self.heads):
            main -= jnp.where(lane >= h * self.main, self.main, 0)
            left -= jnp.where(lane >= low + h * self.rest, self.rest, 0)
        return j * self.size + jnp.where(lane < low, main, left)


def side_order(cols):
    part = HALF_ROWS * cols
    table = np.zeros((round_up(WZ * WH * HALF_COLS, 16), 2 * WZ * part), np.float32)
    for z in range(WZ):
        for r in range(WH):
            low, row = divmod(r, HALF_ROWS)
            for w in range(HALF_COLS):
                table[(z * WH + r) * HALF_COLS + w, (low * WZ + z) * part + row * cols + w] = 1.0
    return table


def window_order(cols, c, out):
    last = c == cols // WW - 1
    part, side = HALF_ROWS * cols, HALF_ROWS * SIDE
    near = 2 * WZ * part
    extra = round_up(WZ * WH * HALF_COLS, 16) if out else 2 * WZ * side
    table = np.zeros((WT, near + last * extra), np.float32)
    for z in range(WZ):
        for r in range(WH):
            for w in range(WW):
                col = c * WW + w + HALF_COLS
                low, row = divmod(r, HALF_ROWS)
                if col < cols:
                    at = (low * WZ + z) * part + row * cols + col
                elif out:
                    at = near + (z * WH + r) * HALF_COLS + col - cols
                else:
                    at = near + (low * WZ + z) * side + row * SIDE + col - cols
                table[(z * WH + r) * WW + w, at] = 1.0
    return table


def send_kernel(tok, cot, inner, below, right, corner):
    levels = tok.shape[0]

    def packed(level, row):
        t, g = tok[level, row].astype(F32), cot[level, row].astype(F32)
        return jnp.concatenate([t[:, :LANES], g[:, :LANES], t[:, LANES:], g[:, LANES:]], axis=1)

    for a in range(levels // WZ):
        at = [(a * WZ + WZ // 2 + z) % levels for z in range(WZ)]
        for whole, side, base in ((below, corner, 0), (inner, right, HALF_ROWS)):
            rows = [packed(level, base + row) for level in at for row in range(HALF_ROWS)]
            whole[a] = jnp.concatenate(rows, axis=0).astype(BF16)
            side[a] = jnp.concatenate([row[:SIDE] for row in rows], axis=0).astype(BF16)


def prep_kernel(chunks, lat_count, bias, bias_t):
    level_windows = bias.shape[0]
    last_lat = lax.axis_index("lat") == lat_count - 1
    me = lax.axis_index("lon")
    parts, size, main = chunks.parts, chunks.size, chunks.main

    def labels(index, window):
        level_label = (index >= LEVEL) & (window == level_windows - 1)
        in_level = jnp.where(index >= LEVEL, index - LEVEL, index)
        row_label = (in_level >= LEVEL // 2) & last_lat
        return level_label.astype(jnp.int32) * 2 + row_label.astype(jnp.int32)

    key_index = lax.broadcasted_iota(jnp.int32, (WT, chunks.width), 0)
    for window in range(level_windows):
        key_labels = labels(key_index, window)
        for j in range(parts):
            heads = range(chunks.heads)
            low = j * size
            rows = []
            if main:
                rows += [bias[window, h, low : low + main, :] for h in heads]
            if chunks.rest:
                rows += [bias[window, h, low + main : low + size, :] for h in heads]
            spare = chunks.width - chunks.heads * size
            if spare:
                rows.append(jnp.zeros((spare, WT), F32))
            turned = jnp.transpose(jnp.concatenate(rows, axis=0)) * LOG2E
            allowed = key_labels == labels(chunks.columns(j), window)
            bias_t[window, lax.rem(j - me + parts, parts)] = jnp.where(allowed, turned, -1e30)


def head_masks(chunks, channels):
    head_dim = channels // chunks.heads
    lane_head = lax.broadcasted_iota(jnp.int32, (1, channels), 1) // head_dim
    lanes = [lane_head == h for h in range(chunks.heads)]
    rest = None
    if chunks.rest:
        row = lax.broadcasted_iota(jnp.int32, (chunks.rest_rows, channels), 0)
        lane = lax.broadcasted_iota(jnp.int32, (chunks.rest_rows, channels), 1) // head_dim
        rest = jnp.zeros((chunks.rest_rows, channels), F32)
        for h in range(chunks.heads):
            inside = (row >= h * chunks.rest) & (row < (h + 1) * chunks.rest) & (lane == h)
            rest = jnp.where(inside, 1.0, rest)
    return lanes, rest


def stack_heads(chunks, value, d, lane_masks, rest_mask):
    low = d * chunks.rows
    main = value[low : low + chunks.main]
    pieces = [main * mask for mask in lane_masks] if chunks.main else []
    if chunks.rest:
        pieces.append(value[low + chunks.main : low + chunks.rows] * rest_mask)
    if chunks.width > chunks.used:
        pieces.append(jnp.zeros((chunks.width - chunks.used, value.shape[1]), value.dtype))
    return jnp.concatenate(pieces, axis=0)


def split(inproj):
    channels = inproj.shape[0]
    return [inproj[:, part * channels : (part + 1) * channels] for part in range(3)]


def rolled(ref, parts):
    me = lax.axis_index("lon")
    return jnp.concatenate([ref[lax.rem(me + d, parts)] for d in range(parts)], axis=0)


def scores_kernel(chunks, near, first, last, *refs):
    pieces, refs = refs[:near], refs[near:]
    gain_ref, inproj, outproj, bias_t, perm, queries, *refs = refs
    weights = split(inproj)
    before = None
    if not first:
        before, *refs = refs
    standard_out, scale_out, keys_out, query_out, up_out, p_out, ds_out, *totals = refs
    parts, width = chunks.parts, chunks.width
    channels = outproj.shape[0]
    spare = channels - LANES
    scaling = (channels // chunks.heads) ** (-0.5)
    lanes, rest_mask = head_masks(chunks, channels)
    lanes = [mask.astype(F32).astype(BF16) for mask in lanes]
    rest_mask = rest_mask.astype(BF16) if chunks.rest else None
    choose = rolled(queries, parts)
    level_windows = pieces[0].shape[0]
    ts, gs = [], []
    for a in range(level_windows):
        moved = dot(perm[...], jnp.concatenate([piece[a] for piece in pieces], axis=0))
        ts.append(jnp.concatenate([moved[:, :LANES], moved[:, 2 * LANES : 2 * LANES + spare]], axis=1))
        gs.append(jnp.concatenate([moved[:, LANES : 2 * LANES], moved[:, 2 * LANES + spare :]], axis=1))
    t = jnp.concatenate(ts, axis=0)
    g = jnp.concatenate(gs, axis=0).astype(BF16)
    centred = t - jnp.mean(t, axis=-1, keepdims=True)
    inverse_rms = lax.rsqrt(jnp.mean(centred * centred, axis=-1, keepdims=True) + epsilon)
    standard = centred * inverse_rms
    standard_out[...] = standard
    scale_out[...] = jnp.broadcast_to(inverse_rms, scale_out.shape)
    normed = (standard * gain_ref[...]).astype(BF16)
    q = dot(normed, weights[0]).astype(BF16)
    k = dot(normed, weights[1]).astype(BF16)
    v = dot(normed, weights[2]).astype(BF16)
    u = dot_nt(g, outproj[...]).astype(BF16)
    keys_out[...] = k
    for a in range(level_windows):
        cut = slice(a * WT, (a + 1) * WT)
        query = dot(choose, q[cut]).astype(BF16)
        up = dot(choose, u[cut]).astype(BF16)
        query_out[a] = query
        up_out[a] = up
        for d in range(parts):
            at = slice(d * width, (d + 1) * width)
            s = dot_nt(k[cut], stack_heads(chunks, query, d, lanes, rest_mask))
            dp = dot_nt(v[cut], stack_heads(chunks, up, d, lanes, rest_mask))
            e = jnp.exp2(s * (scaling * LOG2E) + bias_t[a, d])
            p = e * (1.0 / jnp.sum(e, axis=0, keepdims=True))
            ds = p * (dp - jnp.sum(p * dp, axis=0, keepdims=True))
            p_out[a, :, at] = p.astype(BF16)
            ds_out[a, :, at] = ds.astype(BF16)
            if not first:
                ds += before[a, d]
            if last:
                totals[d][a] = ds.astype(BF16)
            else:
                totals[0][a, d] = ds


def tokens_kernel(chunks, near, first, *refs):
    standard_in, scale_in, keys, queries_in, ups, p_in, ds_in, gain_ref, inproj, perm_t, queries, *refs = refs
    weights = split(inproj)
    before = None
    if not first:
        before, refs = refs[:2], refs[2:]
    outs = refs
    parts, width = chunks.parts, chunks.width
    channels = keys.shape[-1]
    scaling = (channels // chunks.heads) ** (-0.5)
    lanes, rest_mask = head_masks(chunks, channels)
    low_lanes = [mask.astype(F32).astype(BF16) for mask in lanes]
    low_rest = rest_mask.astype(BF16) if chunks.rest else None
    choose_t = jnp.transpose(rolled(queries, parts).astype(F32)).astype(BF16)
    level_windows = p_in.shape[0]
    dqs, dks, dvs = [], [], []
    for a in range(level_windows):
        query, up = queries_in[a], ups[a]
        qs = jnp.concatenate(
            [stack_heads(chunks, query, d, low_lanes, low_rest) for d in range(parts)], axis=0
        )
        us = jnp.concatenate(
            [stack_heads(chunks, up, d, low_lanes, low_rest) for d in range(parts)], axis=0
        )
        ds = ds_in[a]
        dks.append((dot(ds, qs) * scaling).astype(BF16))
        dvs.append(dot(p_in[a], us).astype(BF16))
        flat = dot(jnp.transpose(ds), keys[a * WT : (a + 1) * WT])
        rows = []
        for d in range(parts):
            base = d * width
            if chunks.main:
                picked = flat[base : base + chunks.main]
                for h in range(1, chunks.heads):
                    low = base + h * chunks.main
                    picked = jnp.where(lanes[h], flat[low : low + chunks.main], picked)
                rows.append(picked)
            if chunks.rest:
                low = base + chunks.heads * chunks.main
                rows.append(flat[low : low + chunks.rest_rows] * rest_mask)
        picked = (jnp.concatenate(rows, axis=0) * scaling).astype(BF16)
        dqs.append(dot(choose_t, picked).astype(BF16))
    dq, dk, dv = (jnp.concatenate(parts_of, axis=0) for parts_of in (dqs, dks, dvs))
    scaled = (dot_nt(dq, weights[0]) + dot_nt(dk, weights[1]) + dot_nt(dv, weights[2])) * gain_ref[...]
    standard = standard_in[...]
    inverse_rms = scale_in[:, :1]
    grad = inverse_rms * (
        scaled
        - jnp.mean(scaled, axis=-1, keepdims=True)
        - standard * jnp.mean(scaled * standard, axis=-1, keepdims=True)
    )
    grad = grad.astype(BF16)
    for a in range(level_windows):
        spread = dot(perm_t[...], grad[a * WT : (a + 1) * WT])
        base = 0
        for i, out in enumerate(outs):
            rows = out.shape[1]
            part = spread[base : base + rows]
            if not first and i < 2:
                part += before[i][a].astype(F32)
            out[a] = part.astype(BF16)
            base += rows


def merge_kernel(inner_in, below_in, side, order_t, inner, below):
    half = inner.shape[1]
    lows = []
    for a in range(inner.shape[0]):
        spread = dot(order_t[...], side[a])
        inner[a] = (inner_in[a].astype(F32) + spread[:half]).astype(BF16)
        lows.append(below_in[a].astype(F32) + spread[half:])
    packed = [low[:, :LANES] for low in lows] + [low[:, LANES:] for low in lows]
    below[...] = jnp.concatenate(packed, axis=1).astype(BF16)


def join_kernel(inner, below, grad_input, joined):
    joined[...] = jnp.zeros(joined.shape, F32)
    levels, _, cols, channels = grad_input.shape
    level_windows = levels // WZ
    whole = below[...].astype(F32)
    for a in range(level_windows):
        rest_at = level_windows * LANES + a * (channels - LANES)
        low = jnp.concatenate(
            [whole[:, a * LANES : (a + 1) * LANES], whole[:, rest_at : rest_at + channels - LANES]], axis=1
        )
        high = inner[a].astype(F32)
        for z in range(WZ):
            level = (a * WZ + WZ // 2 + z) % levels
            for row in range(HALF_ROWS):
                at = slice((z * HALF_ROWS + row) * cols, (z * HALF_ROWS + row + 1) * cols)
                grad_input[level, row] = low[at].astype(BF16)
                grad_input[level, HALF_ROWS + row] = high[at].astype(BF16)


def bias_kernel(chunks, joined, *refs):
    arrived, bias_grad = refs[:-1], refs[-1]
    main, rest, heads = chunks.main, chunks.rest, chunks.heads
    for a in range(arrived[0].shape[0]):
        total = arrived[0][a].astype(F32)
        for other in arrived[1:]:
            total += other[a].astype(F32)
        turned = jnp.transpose(total)
        for h in range(heads):
            at = (a * heads + h) * chunks.size
            if main:
                bias_grad[at : at + main, 0, :] = turned[h * main : (h + 1) * main]
            if rest:
                low = heads * main + h * rest
                bias_grad[at + main : at + chunks.size, 0, :] = turned[low : low + rest]


def vmem(count):
    return [pl.BlockSpec(memory_space=pltpu.VMEM)] * count


def call(kernel, outs, args, flops=0):
    return pl.pallas_call(
        kernel,
        out_shape=outs,
        in_specs=vmem(len(args)),
        out_specs=vmem(len(outs)),
        compiler_params=pltpu.CompilerParams(vmem_limit_bytes=40 * 2**20),
        cost_estimate=pl.CostEstimate(flops=flops, bytes_accessed=0, transcendentals=0),
    )(*args)


def shift(value, rows, cols):
    lat_count, lon_count = lax.axis_size("lat"), lax.axis_size("lon")
    pairs = []
    for i in range(lat_count):
        for j in range(lon_count):
            to = (i + rows) % lat_count * lon_count + (j + cols) % lon_count
            pairs.append((i * lon_count + j, to))
    return lax.ppermute(value, ("lat", "lon"), pairs)


def local(tokens, cotangent, norm_gain, inproj_weight, outproj_weight, bias):
    levels, rows, cols, channels = tokens.shape
    level_windows, _, heads = bias.shape[:3]
    lat_count, lon_count = lax.axis_size("lat"), lax.axis_size("lon")
    chunks = Chunks(lon_count, heads)
    windows = cols // WW
    struct = jax.ShapeDtypeStruct
    half, side = WZ * HALF_ROWS * cols, WZ * HALF_ROWS * SIDE
    gain = norm_gain.reshape(1, channels)
    side_table = side_order(cols)
    queries = jnp.asarray(chunks.queries(), BF16)

    inner, below, right, corner = call(
        send_kernel,
        [struct((level_windows, size, 2 * channels), BF16) for size in (half, half, side, side)],
        (tokens, cotangent),
    )
    below = shift(below, -1, 0)
    right = shift(right, 0, -1)
    corner = shift(corner, -1, -1)
    (bias_t,) = call(
        functools.partial(prep_kernel, chunks, lat_count),
        [struct((level_windows, lon_count, WT, chunks.width), F32)],
        (bias.reshape(level_windows, heads, WT, WT),),
        flops=10**9,
    )
    per_window = []
    total = []
    for c in range(windows):
        last = c == windows - 1
        pieces = (inner, below) + ((right, corner) if last else ())
        if last:
            sums = [struct((level_windows, WT, chunks.width), BF16)] * lon_count
        else:
            sums = [struct((level_windows, lon_count, WT, chunks.width), F32)]
        order = jnp.asarray(window_order(cols, c, False), BF16)
        results = call(
            functools.partial(scores_kernel, chunks, len(pieces), c == 0, last),
            [
                struct((level_windows * WT, channels), F32),
                struct((level_windows * WT, LANES), F32),
                struct((level_windows * WT, channels), BF16),
                struct((level_windows, lon_count * chunks.rows, channels), BF16),
                struct((level_windows, lon_count * chunks.rows, channels), BF16),
                struct((level_windows, WT, lon_count * chunks.width), BF16),
                struct((level_windows, WT, lon_count * chunks.width), BF16),
            ]
            + sums,
            (*pieces, gain, inproj_weight, outproj_weight, bias_t, order, queries, *total),
            flops=10**9,
        )
        per_window.append(results[:7])
        total = results[7:]
    arrived = [total[0]] + [shift(total[d], 0, d) for d in range(1, lon_count)]
    grads = []
    for c in reversed(range(windows)):
        last = c == windows - 1
        outs = [struct((level_windows, half, channels), BF16)] * 2
        if last:
            outs.append(struct((level_windows, side_table.shape[0], channels), BF16))
        order = jnp.asarray(window_order(cols, c, True).T, BF16)
        results = call(
            functools.partial(tokens_kernel, chunks, 2, last),
            outs,
            (*per_window[c], gain, inproj_weight, order, queries, *grads),
        )
        grads = results[:2]
        if last:
            left = shift(results[2], 0, 1)
    g_inner, g_below = call(
        merge_kernel,
        [struct((level_windows, half, channels), BF16), struct((half, level_windows * channels), BF16)],
        (*grads, left, jnp.asarray(side_table.T, BF16)),
    )
    above = shift(g_below, 1, 0)
    grad_input, joined = call(
        join_kernel, [struct(tokens.shape, BF16), struct((8, LANES), F32)], (g_inner, above)
    )
    (bias_grad,) = call(
        functools.partial(bias_kernel, chunks),
        [struct((level_windows * heads * chunks.size, 1, WT), F32)],
        (joined, *arrived),
    )
    bias_grad = bias_grad.reshape(level_windows, heads, chunks.size, 1, WT)
    return grad_input, jnp.transpose(bias_grad, (0, 3, 1, 2, 4))


def solution(mesh):
    placed = (
        P(None, "lat", "lon", None),
        P(None, "lat", "lon", None),
        P(),
        P(),
        P(),
        P(None, "lat", None, None, None),
    )
    return jax.shard_map(
        local,
        mesh=mesh,
        in_specs=placed,
        out_specs=(P(None, "lat", "lon", None), P(None, "lat", None, "lon", None)),
        check_vma=False,
    )
```

profile of v0, /device:TPU:0, one launch (start us, length us, event | category | flops | bytes accessed | tf_op | source)
XLA Modules:
  0.0 32.8 jit_solution(8262334727462152850)
XLA Ops:
  0.6 0.0 copy-start.2
  0.6 1.0 %copy-done.2 = bf16[4,6,24,192]{3,2,1,0:T(8,128)(2,1)S(1)} copy-done((bf16[4,6,24,192]{3,2,1,0:T(8,128)(2,1)S(1)}, bf16[4,6,24,192]{3,2,1,0:T(8,128)(2,1)}, u32[]{:S(2)}) %copy-start.2) | copy-done | bytes 221208
  1.6 0.0 copy-start.3
  1.6 1.0 %copy-done.3 = bf16[4,6,24,192]{3,2,1,0:T(8,128)(2,1)S(1)} copy-done((bf16[4,6,24,192]{3,2,1,0:T(8,128)(2,1)S(1)}, bf16[4,6,24,192]{3,2,1,0:T(8,128)(2,1)}, u32[]{:S(2)}) %copy-start.3) | copy-done | bytes 221208
  2.6 0.1 shard_map.131
  2.7 4.5 %collective-permute-start = (bf16[2,144,384]{2,1,0:T(8,128)(2,1)S(1)}, bf16[2,144,384]{2,1,0:T(8,128)(2,1)S(1)}, u32[]{:S(2)}, u32[]{:S(2)}) collective-permute-start(bf16[2,144,384]{2,1,0:T(8,128)(2,1)S(1)} %get-tuple-element.35), channel_id=1, source_target_pairs={{0,28},{1,29},{2,30},{3,31},{4,0},{5,1},{6,2},{7,3},{8,4},{9,5},{1... | collective-permute-start | bytes 663560 | tf_op jit(solution)/shard_map/ppermute | solution.py:375
  7.2 2.4 %collective-permute-start.1 = (bf16[2,48,384]{2,1,0:T(8,128)(2,1)S(1)}, bf16[2,48,384]{2,1,0:T(8,128)(2,1)S(1)}, u32[]{:S(2)}, u32[]{:S(2)}) collective-permute-start(bf16[2,48,384]{2,1,0:T(8,128)(2,1)S(1)} %get-tuple-element.43), channel_id=1, source_target_pairs={{0,3},{1,0},{2,1},{3,2},{4,7},{5,4},{6,5},{7,6},{8,11},{9,8},{10,9... | collective-permute-start | bytes 221192 | tf_op jit(solution)/shard_map/ppermute | solution.py:375
  9.7 0.4 %collective-permute-start.2 = (bf16[2,48,384]{2,1,0:T(8,128)(2,1)S(1)}, bf16[2,48,384]{2,1,0:T(8,128)(2,1)S(1)}, u32[]{:S(2)}, u32[]{:S(2)}) collective-permute-start(bf16[2,48,384]{2,1,0:T(8,128)(2,1)S(1)} %get-tuple-element.44), channel_id=1, source_target_pairs={{0,31},{1,28},{2,29},{3,30},{4,3},{5,0},{6,1},{7,2},{8,7},{9,4},{1... | collective-permute-start | bytes 221192 | tf_op jit(solution)/shard_map/ppermute | solution.py:375
  10.0 0.0 copy-start.8
  10.0 1.5 %copy-done.8 = f32[2,1,6,144,144]{4,3,2,1,0:T(8,128)S(1)} copy-done((f32[2,1,6,144,144]{4,3,2,1,0:T(8,128)S(1)}, f32[2,1,6,144,144]{4,3,2,1,0:T(8,128)}, u32[]{:S(2)}) %copy-start.8) | copy-done | bytes 995352
  11.5 0.0 copy-start
  11.5 0.0 copy-start.1
  11.5 0.0 copy-start.7
  11.5 0.0 copy-start.9
  11.5 0.0 copy-start.11
  11.5 0.6 %shard_map.132.refs_5_.refs_7_ = f32[2,4,144,256]{3,2,1,0:T(8,128)S(1)} custom-call(f32[2,6,144,144]{3,2,1,0:T(8,128)S(1)} %bitcast.7), custom_call_target="tpu_custom_call" | custom-call | flops 1000000000 | tf_op jit(solution)/shard_map/pallas_call | solution.py:358
  12.1 0.0 collective-permute-done.refs_1_
  12.1 0.3 %copy-done = bf16[192,576]{1,0:T(8,128)(2,1)S(1)} copy-done((bf16[192,576]{1,0:T(8,128)(2,1)S(1)}, bf16[192,576]{1,0:T(8,128)(2,1)}, u32[]{:S(2)}) %copy-start) | copy-done | bytes 221208
  12.4 0.1 copy-done.1
  12.5 0.0 copy-done.7
  12.5 0.1 copy-done.9
  12.6 0.1 copy-done.11
  12.7 0.0 copy-start.10
  12.7 1.7 %shard_map.133 = (f32[288,192]{1,0:T(8,128)S(1)}, f32[288,128]{1,0:T(8,128)S(1)}, bf16[288,192]{1,0:T(8,128)(2,1)S(1)}, bf16[2,256,192]{2,1,0:T(8,128)(2,1)S(1)}...) custom-call(bf16[2,144,384]{2,1,0:T(8,128)(2,1)S(1)} %get-tuple-elem, ...), custom_call_target="tpu_custom_call" | custom-call | flops 1000000000 | tf_op jit(solution)/shard_map/pallas_call | solution.py:358
  14.4 0.0 collective-permute-done.1.refs_2_
  14.4 0.0 collective-permute-done.2.refs_3_
  14.4 0.0 copy-done.10
  14.4 0.0 copy-start.4
  14.5 1.8 %shard_map.134 = (f32[288,192]{1,0:T(8,128)S(1)}, f32[288,128]{1,0:T(8,128)S(1)}, bf16[288,192]{1,0:T(8,128)(2,1)S(1)}, bf16[2,256,192]{2,1,0:T(8,128)(2,1)S(1)}...) custom-call(bf16[2,144,384]{2,1,0:T(8,128)(2,1)S(1)} %get-tuple-elem, ...), custom_call_target="tpu_custom_call" | custom-call | flops 1000000000 | tf_op jit(solution)/shard_map/pallas_call | solution.py:358
  16.3 0.0 copy-done.4
  16.3 0.0 copy-start.5
  16.3 1.7 %shard_map.135 = (bf16[2,144,192]{2,1,0:T(8,128)(2,1)S(1)}, bf16[2,144,192]{2,1,0:T(8,128)(2,1)S(1)}, bf16[2,80,192]{2,1,0:T(8,128)(2,1)S(1)}) custom-call(f32[288,192]{1,0:T(8,128)S(1)} %get-tuple-element.46.refs_0_, f32[288,128]{1,0:T(8,128)S(1)} %get-tuple-element.47.refs_1_, bf16[288,192]{1,0:T(8,128)(2,1)S(1)} %get-tuple-element.48.refs_2_, ...), custom_call_target="tpu_custom_call" | custom-call | tf_op jit(solution)/shard_map/pallas_call | solution.py:358
  18.0 1.5 %collective-permute-start.3 = (bf16[2,80,192]{2,1,0:T(8,128)(2,1)S(1)}, bf16[2,80,192]{2,1,0:T(8,128)(2,1)S(1)}, u32[]{:S(2)}, u32[]{:S(2)}) collective-permute-start(bf16[2,80,192]{2,1,0:T(8,128)(2,1)S(1)} %get-tuple-element.57), channel_id=1, source_target_pairs={{0,1},{1,2},{2,3},{3,0},{4,5},{5,6},{6,7},{7,4},{8,9},{9,10},{10,1... | collective-permute-start | bytes 184328 | tf_op jit(solution)/shard_map/ppermute | solution.py:375
  19.5 0.5 %collective-permute-start.5 = (bf16[2,144,256]{2,1,0:T(8,128)(2,1)S(1)}, bf16[2,144,256]{2,1,0:T(8,128)(2,1)S(1)}, u32[]{:S(2)}, u32[]{:S(2)}) collective-permute-start(bf16[2,144,256]{2,1,0:T(8,128)(2,1)S(1)} %get-tuple-element.63), channel_id=1, source_target_pairs={{0,1},{1,2},{2,3},{3,0},{4,5},{5,6},{6,7},{7,4},{8,9},{9,10},{10,1... | collective-permute-start | bytes 442376 | tf_op jit(solution)/shard_map/ppermute | solution.py:375
  20.0 1.5 %collective-permute-start.6 = (bf16[2,144,256]{2,1,0:T(8,128)(2,1)S(1)}, bf16[2,144,256]{2,1,0:T(8,128)(2,1)S(1)}, u32[]{:S(2)}, u32[]{:S(2)}) collective-permute-start(bf16[2,144,256]{2,1,0:T(8,128)(2,1)S(1)} %get-tuple-element.64), channel_id=1, source_target_pairs={{0,2},{1,3},{2,0},{3,1},{4,6},{5,7},{6,4},{7,5},{8,10},{9,11},{10,... | collective-permute-start | bytes 442376 | tf_op jit(solution)/shard_map/ppermute | solution.py:375
  21.5 1.4 %collective-permute-start.7 = (bf16[2,144,256]{2,1,0:T(8,128)(2,1)S(1)}, bf16[2,144,256]{2,1,0:T(8,128)(2,1)S(1)}, u32[]{:S(2)}, u32[]{:S(2)}) collective-permute-start(bf16[2,144,256]{2,1,0:T(8,128)(2,1)S(1)} %get-tuple-element.65), channel_id=1, source_target_pairs={{0,3},{1,0},{2,1},{3,2},{4,7},{5,4},{6,5},{7,6},{8,11},{9,8},{10,9... | collective-permute-start | bytes 442376 | tf_op jit(solution)/shard_map/ppermute | solution.py:375
  23.0 0.0 copy-done.5
  23.0 1.6 %shard_map.136 = (bf16[2,144,192]{2,1,0:T(8,128)(2,1)S(1)}, bf16[2,144,192]{2,1,0:T(8,128)(2,1)S(1)}) custom-call(f32[288,192]{1,0:T(8,128)S(1)} %get-tuple-element.36.refs_0_, f32[288,128]{1,0:T(8,128)S(1)} %get-tuple-element.37.refs_1_, bf16[288,192]{1,0:T(8,128)(2,1)S(1)} %get-tuple-element.38.refs_2_, ...), custom_call_target="tpu_custom_call" | custom-call | tf_op jit(solution)/shard_map/pallas_call | solution.py:358
  24.6 0.0 collective-permute-done.3.side
  24.6 0.0 copy-done.6
  24.7 0.3 shard_map.137
  24.9 0.1 collective-permute-start.4
  25.0 6.0 %collective-permute-done.4.below = bf16[144,384]{1,0:T(8,128)(2,1)S(1)} collective-permute-done((bf16[144,384]{1,0:T(8,128)(2,1)S(1)}, bf16[144,384]{1,0:T(8,128)(2,1)S(1)}, u32[]{:S(2)}, u32[]{:S(2)}) %collective-permute-start.4) | collective-permute-done | bytes 110624 | tf_op jit(solution)/shard_map/ppermute | solution.py:375
  31.0 0.8 %shard_map.138 = (bf16[4,6,24,192]{3,2,1,0:T(8,128)(2,1)}, f32[8,128]{1,0:T(8,128)S(1)}) custom-call(bf16[2,144,192]{2,1,0:T(8,128)(2,1)S(1)} %get-tuple-element.58.inner, bf16[144,384]{1,0:T(8,128)(2,1)S(1)} %collective-permute-done.4.below), custom_call_target="tpu_custom_call" | custom-call | tf_op jit(solution)/shard_map/pallas_call | solution.py:358
  31.8 0.0 collective-permute-done.5.refs_1_
  31.8 0.0 collective-permute-done.6.refs_2_
  31.8 0.0 collective-permute-done.7.refs_3_
  31.8 1.0 %shard_map.139 = f32[432,1,144]{2,1,0:T(1,128)} custom-call(f32[8,128]{1,0:T(8,128)S(1)} %get-tuple-element.61.joined, bf16[2,144,256]{2,1,0:T(8,128)(2,1)S(1)} %get-tuple-element.62.refs_0_, bf16[2,144,256]{2,1,0:T(8,128)(2,1)S(1)} %collective-permute-done.5.refs_1_, bf16[2,144,256]{2,1,0:T(8,128)(2,1)S(1)} %collective-permute-done.6.refs_2_, ...), custom_call_target="tpu_custom_call" | custom-call | tf_op jit(solution)/shard_map/pallas_call | solution.py:358
  (1 shorter events, 0.0 us)
Async XLA Ops:
  0.6 1.0 %copy-start.2 = (bf16[4,6,24,192]{3,2,1,0:T(8,128)(2,1)S(1)}, bf16[4,6,24,192]{3,2,1,0:T(8,128)(2,1)}, u32[]{:S(2)}) copy-start(bf16[4,6,24,192]{3,2,1,0:T(8,128)(2,1)} %tok.1) | copy-start | bytes 663556
  1.6 1.0 %copy-start.3 = (bf16[4,6,24,192]{3,2,1,0:T(8,128)(2,1)S(1)}, bf16[4,6,24,192]{3,2,1,0:T(8,128)(2,1)}, u32[]{:S(2)}) copy-start(bf16[4,6,24,192]{3,2,1,0:T(8,128)(2,1)} %cot.1) | copy-start | bytes 663556
  2.7 9.4 %collective-permute-start = (bf16[2,144,384]{2,1,0:T(8,128)(2,1)S(1)}, bf16[2,144,384]{2,1,0:T(8,128)(2,1)S(1)}, u32[]{:S(2)}, u32[]{:S(2)}) collective-permute-start(bf16[2,144,384]{2,1,0:T(8,128)(2,1)S(1)} %get-tuple-element.35), channel_id=1, source_target_pairs={{0,28},{1,29},{2,30},{3,31},{4,0},{5,1},{6,2},{7,3},{8,4},{9,5},{1... | collective-permute-start | bytes 663560 | tf_op jit(solution)/shard_map/ppermute | solution.py:375
  7.2 7.2 %collective-permute-start.1 = (bf16[2,48,384]{2,1,0:T(8,128)(2,1)S(1)}, bf16[2,48,384]{2,1,0:T(8,128)(2,1)S(1)}, u32[]{:S(2)}, u32[]{:S(2)}) collective-permute-start(bf16[2,48,384]{2,1,0:T(8,128)(2,1)S(1)} %get-tuple-element.43), channel_id=1, source_target_pairs={{0,3},{1,0},{2,1},{3,2},{4,7},{5,4},{6,5},{7,6},{8,11},{9,8},{10,9... | collective-permute-start | bytes 221192 | tf_op jit(solution)/shard_map/ppermute | solution.py:375
  9.7 4.8 %collective-permute-start.2 = (bf16[2,48,384]{2,1,0:T(8,128)(2,1)S(1)}, bf16[2,48,384]{2,1,0:T(8,128)(2,1)S(1)}, u32[]{:S(2)}, u32[]{:S(2)}) collective-permute-start(bf16[2,48,384]{2,1,0:T(8,128)(2,1)S(1)} %get-tuple-element.44), channel_id=1, source_target_pairs={{0,31},{1,28},{2,29},{3,30},{4,3},{5,0},{6,1},{7,2},{8,7},{9,4},{1... | collective-permute-start | bytes 221192 | tf_op jit(solution)/shard_map/ppermute | solution.py:375
  10.0 1.5 %copy-start.8 = (f32[2,1,6,144,144]{4,3,2,1,0:T(8,128)S(1)}, f32[2,1,6,144,144]{4,3,2,1,0:T(8,128)}, u32[]{:S(2)}) copy-start(f32[2,1,6,144,144]{4,3,2,1,0:T(8,128)} %param.17) | copy-start | bytes 2985988
  11.5 0.9 %copy-start = (bf16[192,576]{1,0:T(8,128)(2,1)S(1)}, bf16[192,576]{1,0:T(8,128)(2,1)}, u32[]{:S(2)}) copy-start(bf16[192,576]{1,0:T(8,128)(2,1)} %refs_8_.4) | copy-start | bytes 663556
  11.5 1.0 %copy-start.1 = (bf16[4,64,144]{2,1,0:T(8,128)(2,1)S(1)}, bf16[4,64,144]{2,1,0:T(8,128)(2,1)}, u32[]{:S(2)}) copy-start(bf16[4,64,144]{2,1,0:T(8,128)(2,1)} %constant.12.clone.refs_7_.refs_9_.refs_10_) | copy-start | bytes 221188
  11.5 1.0 %copy-start.7 = (f32[192]{0:T(256)S(1)}, f32[192]{0:T(256)}, u32[]{:S(2)}) copy-start(f32[192]{0:T(256)} %param.14) | copy-start | bytes 2308
  11.5 1.1 %copy-start.9 = (bf16[192,192]{1,0:T(8,128)(2,1)S(1)}, bf16[192,192]{1,0:T(8,128)(2,1)}, u32[]{:S(2)}) copy-start(bf16[192,192]{1,0:T(8,128)(2,1)} %refs_6_.2) | copy-start | bytes 221188
  11.5 1.1 %copy-start.11 = (bf16[144,288]{1,0:T(8,128)(2,1)S(1)}, bf16[144,288]{1,0:T(8,128)(2,1)}, u32[]{:S(2)}) copy-start(bf16[144,288]{1,0:T(8,128)(2,1)} %constant.13.clone.refs_6_) | copy-start | bytes 248836
  12.7 1.8 %copy-start.10 = (bf16[144,384]{1,0:T(8,128)(2,1)S(1)}, bf16[144,384]{1,0:T(8,128)(2,1)}, u32[]{:S(2)}) copy-start(bf16[144,384]{1,0:T(8,128)(2,1)} %constant.14.clone.refs_8_) | copy-start | bytes 331780
  14.4 1.9 %copy-start.4 = (bf16[368,144]{1,0:T(8,128)(2,1)S(1)}, bf16[368,144]{1,0:T(8,128)(2,1)}, u32[]{:S(2)}) copy-start(bf16[368,144]{1,0:T(8,128)(2,1)} %constant.15.clone.refs_9_) | copy-start | bytes 317956
  16.3 6.7 %copy-start.5 = (bf16[288,144]{1,0:T(8,128)(2,1)S(1)}, bf16[288,144]{1,0:T(8,128)(2,1)}, u32[]{:S(2)}) copy-start(bf16[288,144]{1,0:T(8,128)(2,1)} %constant.16.clone.refs_9_) | copy-start | bytes 248836
  18.0 6.6 %collective-permute-start.3 = (bf16[2,80,192]{2,1,0:T(8,128)(2,1)S(1)}, bf16[2,80,192]{2,1,0:T(8,128)(2,1)S(1)}, u32[]{:S(2)}, u32[]{:S(2)}) collective-permute-start(bf16[2,80,192]{2,1,0:T(8,128)(2,1)S(1)} %get-tuple-element.57), channel_id=1, source_target_pairs={{0,1},{1,2},{2,3},{3,0},{4,5},{5,6},{6,7},{7,4},{8,9},{9,10},{10,1... | collective-permute-start | bytes 184328 | tf_op jit(solution)/shard_map/ppermute | solution.py:375
  19.5 12.2 %collective-permute-start.5 = (bf16[2,144,256]{2,1,0:T(8,128)(2,1)S(1)}, bf16[2,144,256]{2,1,0:T(8,128)(2,1)S(1)}, u32[]{:S(2)}, u32[]{:S(2)}) collective-permute-start(bf16[2,144,256]{2,1,0:T(8,128)(2,1)S(1)} %get-tuple-element.63), channel_id=1, source_target_pairs={{0,1},{1,2},{2,3},{3,0},{4,5},{5,6},{6,7},{7,4},{8,9},{9,10},{10,1... | collective-permute-start | bytes 442376 | tf_op jit(solution)/shard_map/ppermute | solution.py:375
  20.0 11.7 %collective-permute-start.6 = (bf16[2,144,256]{2,1,0:T(8,128)(2,1)S(1)}, bf16[2,144,256]{2,1,0:T(8,128)(2,1)S(1)}, u32[]{:S(2)}, u32[]{:S(2)}) collective-permute-start(bf16[2,144,256]{2,1,0:T(8,128)(2,1)S(1)} %get-tuple-element.64), channel_id=1, source_target_pairs={{0,2},{1,3},{2,0},{3,1},{4,6},{5,7},{6,4},{7,5},{8,10},{9,11},{10,... | collective-permute-start | bytes 442376 | tf_op jit(solution)/shard_map/ppermute | solution.py:375
  21.5 10.2 %collective-permute-start.7 = (bf16[2,144,256]{2,1,0:T(8,128)(2,1)S(1)}, bf16[2,144,256]{2,1,0:T(8,128)(2,1)S(1)}, u32[]{:S(2)}, u32[]{:S(2)}) collective-permute-start(bf16[2,144,256]{2,1,0:T(8,128)(2,1)S(1)} %get-tuple-element.65), channel_id=1, source_target_pairs={{0,3},{1,0},{2,1},{3,2},{4,7},{5,4},{6,5},{7,6},{8,11},{9,8},{10,9... | collective-permute-start | bytes 442376 | tf_op jit(solution)/shard_map/ppermute | solution.py:375
  23.0 1.7 %copy-start.6 = (bf16[288,80]{1,0:T(8,128)(2,1)S(1)}, bf16[288,80]{1,0:T(8,128)(2,1)}, u32[]{:S(2)}) copy-start(bf16[288,80]{1,0:T(8,128)(2,1)} %constant.17.clone.order_t) | copy-start | bytes 138244
  24.9 6.0 %collective-permute-start.4 = (bf16[144,384]{1,0:T(8,128)(2,1)S(1)}, bf16[144,384]{1,0:T(8,128)(2,1)S(1)}, u32[]{:S(2)}, u32[]{:S(2)}) collective-permute-start(bf16[144,384]{1,0:T(8,128)(2,1)S(1)} %get-tuple-element.59), channel_id=1, source_target_pairs={{0,4},{1,5},{2,6},{3,7},{4,8},{5,9},{6,10},{7,11},{8,12},{9,13},{1... | collective-permute-start | bytes 331784 | tf_op jit(solution)/shard_map/ppermute | solution.py:375
where the time goes:
time: 33 us; the launch traced here: 32.8 us
  starting transfers between devices  12.4 us (38%)
  Pallas kernels  9.67 us (29%)
  waiting for transfers between devices  5.98 us (18%)
  local copies, waits for them, and re-layouts  3.96 us (12%)
  between operations  0.78 us (2%)
    ppermute x8, starting transfers between devices, shift(): return lax.ppermute(value, ('lat', 'lon'), pairs)  12.4 us
    pallas_call x9, Pallas kernels, call(): pl.pallas_call(kernel, out_shape=outs, in_specs=vmem(len(args)), out_spec...  9.67 us
    ppermute x8, waiting for transfers between devices, shift(): return lax.ppermute(value, ('lat', 'lon'), pairs)  5.98 us
    unnamed x24, local copies, waits for them, and re-layouts  3.96 us
  transfers between devices with their start and end apart: 8, of which 1 were waited for; matrix products, arithmetic and copies ran while one was open for 0% of the time, Pallas kernels for 15%

commit v1 on v0

--- a/solution.py
+++ b/solution.py
@@ -67,23 +67,11 @@
         return j * self.size + jnp.where(lane < low, main, left)
 
 
-def side_order(cols):
-    part = HALF_ROWS * cols
-    table = np.zeros((round_up(WZ * WH * HALF_COLS, 16), 2 * WZ * part), np.float32)
-    for z in range(WZ):
-        for r in range(WH):
-            low, row = divmod(r, HALF_ROWS)
-            for w in range(HALF_COLS):
-                table[(z * WH + r) * HALF_COLS + w, (low * WZ + z) * part + row * cols + w] = 1.0
-    return table
-
-
-def window_order(cols, c, out):
+def window_order(cols, c):
     last = c == cols // WW - 1
     part, side = HALF_ROWS * cols, HALF_ROWS * SIDE
     near = 2 * WZ * part
-    extra = round_up(WZ * WH * HALF_COLS, 16) if out else 2 * WZ * side
-    table = np.zeros((WT, near + last * extra), np.float32)
+    table = np.zeros((WT, near + last * 2 * WZ * side), np.float32)
     for z in range(WZ):
         for r in range(WH):
             for w in range(WW):
@@ -91,15 +79,21 @@
                 low, row = divmod(r, HALF_ROWS)
                 if col < cols:
                     at = (low * WZ + z) * part + row * cols + col
-                elif out:
-                    at = near + (z * WH + r) * HALF_COLS + col - cols
                 else:
                     at = near + (low * WZ + z) * side + row * SIDE + col - cols
                 table[(z * WH + r) * WW + w, at] = 1.0
     return table
 
 
-def send_kernel(tok, cot, inner, below, right, corner):
+def send_kernel(tok_hbm, cot_hbm, inner, below, right, corner, tok, cot, sems):
+    copies = [
+        pltpu.make_async_copy(tok_hbm, tok, sems.at[0]),
+        pltpu.make_async_copy(cot_hbm, cot, sems.at[1]),
+    ]
+    for copy in copies:
+        copy.start()
+    for copy in copies:
+        copy.wait()
     levels = tok.shape[0]
 
     def packed(level, row):
@@ -197,6 +191,7 @@
     lanes = [mask.astype(F32).astype(BF16) for mask in lanes]
     rest_mask = rest_mask.astype(BF16) if chunks.rest else None
     choose = rolled(queries, parts)
+    me = lax.axis_index("lon")
     level_windows = pieces[0].shape[0]
     ts, gs = [], []
     for a in range(level_windows):
@@ -234,7 +229,7 @@
             if not first:
                 ds += before[a, d]
             if last:
-                totals[d][a] = ds.astype(BF16)
+                totals[0][lax.rem(me + d, parts), a] = ds.astype(BF16)
             else:
                 totals[0][a, d] = ds
 
@@ -291,31 +286,26 @@
         - standard * jnp.mean(scaled * standard, axis=-1, keepdims=True)
     )
     grad = grad.astype(BF16)
+    lows = []
     for a in range(level_windows):
         spread = dot(perm_t[...], grad[a * WT : (a + 1) * WT])
         base = 0
         for i, out in enumerate(outs):
-            rows = out.shape[1]
+            rows = out.shape[-2]
             part = spread[base : base + rows]
             if not first and i < 2:
                 part += before[i][a].astype(F32)
-            out[a] = part.astype(BF16)
+            if not first and i == 1:
+                lows.append(part)
+            else:
+                out[a] = part.astype(BF16)
             base += rows
-
-
-def merge_kernel(inner_in, below_in, side, order_t, inner, below):
-    half = inner.shape[1]
-    lows = []
-    for a in range(inner.shape[0]):
-        spread = dot(order_t[...], side[a])
-        inner[a] = (inner_in[a].astype(F32) + spread[:half]).astype(BF16)
-        lows.append(below_in[a].astype(F32) + spread[half:])
-    packed = [low[:, :LANES] for low in lows] + [low[:, LANES:] for low in lows]
-    below[...] = jnp.concatenate(packed, axis=1).astype(BF16)
-
-
-def join_kernel(inner, below, grad_input, joined):
-    joined[...] = jnp.zeros(joined.shape, F32)
+    if not first:
+        packed = [low[:, :LANES] for low in lows] + [low[:, LANES:] for low in lows]
+        outs[1][...] = jnp.concatenate(packed, axis=1).astype(BF16)
+
+
+def join_kernel(inner, below, right, corner, after, grad_input):
     levels, _, cols, channels = grad_input.shape
     level_windows = levels // WZ
     whole = below[...].astype(F32)
@@ -324,22 +314,24 @@
         low = jnp.concatenate(
             [whole[:, a * LANES : (a + 1) * LANES], whole[:, rest_at : rest_at + channels - LANES]], axis=1
         )
-        high = inner[a].astype(F32)
+        parts = ((low, corner[a].astype(F32), 0), (inner[a].astype(F32), right[a].astype(F32), HALF_ROWS))
         for z in range(WZ):
             level = (a * WZ + WZ // 2 + z) % levels
             for row in range(HALF_ROWS):
-                at = slice((z * HALF_ROWS + row) * cols, (z * HALF_ROWS + row + 1) * cols)
-                grad_input[level, row] = low[at].astype(BF16)
-                grad_input[level, HALF_ROWS + row] = high[at].astype(BF16)
-
-
-def bias_kernel(chunks, joined, *refs):
-    arrived, bias_grad = refs[:-1], refs[-1]
+                at = z * HALF_ROWS + row
+                for wide, side, base in parts:
+                    first = wide[at * cols : at * cols + SIDE] + side[at * SIDE : (at + 1) * SIDE]
+                    rest = wide[at * cols + SIDE : (at + 1) * cols]
+                    grad_input[level, base + row] = jnp.concatenate([first, rest], axis=0).astype(BF16)
+
+
+def bias_kernel(chunks, arrived, bias_grad, after):
+    after[...] = jnp.zeros(after.shape, F32)
     main, rest, heads = chunks.main, chunks.rest, chunks.heads
-    for a in range(arrived[0].shape[0]):
-        total = arrived[0][a].astype(F32)
-        for other in arrived[1:]:
-            total += other[a].astype(F32)
+    for a in range(arrived.shape[1]):
+        total = arrived[0, a].astype(F32)
+        for d in range(1, chunks.parts):
+            total += arrived[d, a].astype(F32)
         turned = jnp.transpose(total)
         for h in range(heads):
             at = (a * heads + h) * chunks.size
@@ -354,13 +346,14 @@
     return [pl.BlockSpec(memory_space=pltpu.VMEM)] * count
 
 
-def call(kernel, outs, args, flops=0):
+def call(kernel, outs, args, flops=0, specs=None, scratch=(), limit=40):
     return pl.pallas_call(
         kernel,
         out_shape=outs,
-        in_specs=vmem(len(args)),
+        in_specs=specs or vmem(len(args)),
         out_specs=vmem(len(outs)),
-        compiler_params=pltpu.CompilerParams(vmem_limit_bytes=40 * 2**20),
+        scratch_shapes=list(scratch),
+        compiler_params=pltpu.CompilerParams(vmem_limit_bytes=limit * 2**20),
         cost_estimate=pl.CostEstimate(flops=flops, bytes_accessed=0, transcendentals=0),
     )(*args)
 
@@ -384,13 +377,15 @@
     struct = jax.ShapeDtypeStruct
     half, side = WZ * HALF_ROWS * cols, WZ * HALF_ROWS * SIDE
     gain = norm_gain.reshape(1, channels)
-    side_table = side_order(cols)
     queries = jnp.asarray(chunks.queries(), BF16)
 
     inner, below, right, corner = call(
         send_kernel,
         [struct((level_windows, size, 2 * channels), BF16) for size in (half, half, side, side)],
         (tokens, cotangent),
+        specs=[pl.BlockSpec(memory_space=pltpu.HBM)] * 2,
+        scratch=[pltpu.VMEM(tokens.shape, BF16)] * 2 + [pltpu.SemaphoreType.DMA((2,))],
+        limit=56,
     )
     below = shift(below, -1, 0)
     right = shift(right, 0, -1)
@@ -407,10 +402,10 @@
         last = c == windows - 1
         pieces = (inner, below) + ((right, corner) if last else ())
         if last:
-            sums = [struct((level_windows, WT, chunks.width), BF16)] * lon_count
+            sums = [struct((lon_count, level_windows, WT, chunks.width), BF16)]
         else:
             sums = [struct((level_windows, lon_count, WT, chunks.width), F32)]
-        order = jnp.asarray(window_order(cols, c, False), BF16)
+        order = jnp.asarray(window_order(cols, c), BF16)
         results = call(
             functools.partial(scores_kernel, chunks, len(pieces), c == 0, last),
             [
@@ -428,35 +423,31 @@
         )
         per_window.append(results[:7])
         total = results[7:]
-    arrived = [total[0]] + [shift(total[d], 0, d) for d in range(1, lon_count)]
+    arrived = lax.all_to_all(total[0], "lon", 0, 0, tiled=True)
+    wide = struct((level_windows, half, channels), BF16)
+    thin = struct((level_windows, side, channels), BF16)
     grads = []
     for c in reversed(range(windows)):
         last = c == windows - 1
-        outs = [struct((level_windows, half, channels), BF16)] * 2
-        if last:
-            outs.append(struct((level_windows, side_table.shape[0], channels), BF16))
-        order = jnp.asarray(window_order(cols, c, True).T, BF16)
+        order = jnp.asarray(window_order(cols, c).T, BF16)
         results = call(
             functools.partial(tokens_kernel, chunks, 2, last),
-            outs,
+            [wide, wide, thin, thin] if last else [wide, struct((half, level_windows * channels), BF16)],
             (*per_window[c], gain, inproj_weight, order, queries, *grads),
+            flops=10**9 * (not last),
         )
         grads = results[:2]
         if last:
-            left = shift(results[2], 0, 1)
-    g_inner, g_below = call(
-        merge_kernel,
-        [struct((level_windows, half, channels), BF16), struct((half, level_windows * channels), BF16)],
-        (*grads, left, jnp.asarray(side_table.T, BF16)),
-    )
-    above = shift(g_below, 1, 0)
-    grad_input, joined = call(
-        join_kernel, [struct(tokens.shape, BF16), struct((8, LANES), F32)], (g_inner, above)
-    )
-    (bias_grad,) = call(
+            left, corner = shift(results[2], 0, 1), shift(results[3], 1, 1)
+    above = shift(grads[1], 1, 0)
+    bias_grad, after = call(
         functools.partial(bias_kernel, chunks),
-        [struct((level_windows * heads * chunks.size, 1, WT), F32)],
-        (joined, *arrived),
+        [struct((level_windows * heads * chunks.size, 1, WT), F32), struct((8, LANES), F32)],
+        (arrived,),
+        flops=10**9,
+    )
+    (grad_input,) = call(
+        join_kernel, [struct(tokens.shape, BF16)], (grads[0], above, left, corner, after)
     )
     bias_grad = bias_grad.reshape(level_windows, heads, chunks.size, 1, WT)
     return grad_input, jnp.transpose(bias_grad, (0, 3, 1, 2, 4))

time: 33 us -> 37.2 us (1.13)
  Pallas kernels: 9.67 us -> 12.7 us
  starting transfers between devices: 12.4 us -> 13.8 us
  waiting for transfers between devices: 5.98 us -> 5.33 us
    all_to_all x0 -> x1, starting transfers between devices: none -> 3.62 us  [local(): arrived = lax.all_to_all(total[0], 'lon', 0, 0, tiled=True)]
    ppermute x8 -> x6, waiting for transfers between devices: 5.98 us -> 2.43 us  [shift(): return lax.ppermute(value, ('lat', 'lon'), pairs)]
    pallas_call x9 -> x8, Pallas kernels: 9.67 us -> 12.7 us  [call(): pl.pallas_call(kernel, out_shape=outs, in_specs=specs or vmem(len(args)),...]
    all_to_all x0 -> x1, waiting for transfers between devices: none -> 2.91 us  [local(): arrived = lax.all_to_all(total[0], 'lon', 0, 0, tiled=True)]
    ppermute x8 -> x6, starting transfers between devices: 12.4 us -> 10.2 us  [shift(): return lax.ppermute(value, ('lat', 'lon'), pairs)]
    unnamed x24 -> x48, local copies, waits for them, and re-layouts: 3.96 us -> 4.2 us
  transfers between devices with their start and end apart: 8 -> 7, of which waited for: 1 -> 3; matrix products, arithmetic and copies ran while one was open for 0% -> 0% of each run, Pallas kernels for 15% -> 20%
where the time goes in v1:
time: 37.2 us; the launch traced here: 37 us
  starting transfers between devices  13.8 us (37%)
  Pallas kernels  12.7 us (34%)
  waiting for transfers between devices  5.33 us (14%)
  local copies, waits for them, and re-layouts  4.2 us (11%)
  between operations  0.86 us (2%)
    pallas_call x8, Pallas kernels, call(): pl.pallas_call(kernel, out_shape=outs, in_specs=specs or vmem(len(args)),...  12.7 us
    ppermute x6, starting transfers between devices, shift(): return lax.ppermute(value, ('lat', 'lon'), pairs)  10.2 us
    unnamed x48, local copies, waits for them, and re-layouts  4.2 us
    all_to_all x1, starting transfers between devices, local(): arrived = lax.all_to_all(total[0], 'lon', 0, 0, tiled=True)  3.62 us
    all_to_all x1, waiting for transfers between devices, local(): arrived = lax.all_to_all(total[0], 'lon', 0, 0, tiled=True)  2.91 us
    ppermute x6, waiting for transfers between devices, shift(): return lax.ppermute(value, ('lat', 'lon'), pairs)  2.43 us
  transfers between devices with their start and end apart: 7, of which 3 were waited for; matrix products, arithmetic and copies ran while one was open for 0% of the time, Pallas kernels for 20%

profile of v1, /device:TPU:0, one launch (start us, length us, event | category | flops | bytes accessed | tf_op | source)
XLA Modules:
  0.0 37.0 jit_solution(3164954704624511684)
XLA Ops:
  0.6 2.0 %shard_map.122 = (bf16[2,144,384]{2,1,0:T(8,128)(2,1)}, bf16[2,144,384]{2,1,0:T(8,128)(2,1)}, bf16[2,48,384]{2,1,0:T(8,128)(2,1)}, bf16[2,48,384]{2,1,0:T(8,128)(2,1)}) custom-call(bf16[4,6,24,192]{3,2,1,0:T(8,128)(2,1)} %tok_hbm.1, bf16[4,6,24,192]{3,2,1,0:T(8,128)(2,1)} %cot_hbm.1), custom_call_target="tpu_custom_call" | custom-call | tf_op jit(solution)/shard_map/pallas_call | solution.py:350
  2.6 4.5 %collective-permute-start = (bf16[2,144,384]{2,1,0:T(8,128)(2,1)}, bf16[2,144,384]{2,1,0:T(8,128)(2,1)S(1)}, u32[]{:S(2)}, u32[]{:S(2)}) collective-permute-start(bf16[2,144,384]{2,1,0:T(8,128)(2,1)} %get-tuple-element.31), channel_id=1, source_target_pairs={{0,28},{1,29},{2,30},{3,31},{4,0},{5,1},{6,2},{7,3},{8,4},{9,5},{1... | collective-permute-start | bytes 663560 | tf_op jit(solution)/shard_map/ppermute | solution.py:368
  7.2 2.4 %collective-permute-start.1 = (bf16[2,48,384]{2,1,0:T(8,128)(2,1)}, bf16[2,48,384]{2,1,0:T(8,128)(2,1)S(1)}, u32[]{:S(2)}, u32[]{:S(2)}) collective-permute-start(bf16[2,48,384]{2,1,0:T(8,128)(2,1)} %get-tuple-element.39), channel_id=1, source_target_pairs={{0,3},{1,0},{2,1},{3,2},{4,7},{5,4},{6,5},{7,6},{8,11},{9,8},{10,9... | collective-permute-start | bytes 221192 | tf_op jit(solution)/shard_map/ppermute | solution.py:368
  9.6 0.4 collective-permute-start.2
  10.0 1.5 %copy-done.4 = f32[2,1,6,144,144]{4,3,2,1,0:T(8,128)S(1)} copy-done((f32[2,1,6,144,144]{4,3,2,1,0:T(8,128)S(1)}, f32[2,1,6,144,144]{4,3,2,1,0:T(8,128)}, u32[]{:S(2)}) %copy-start.4) | copy-done | bytes 995352
  11.5 0.0 copy-start.6
  11.5 0.0 copy-start.9
  11.5 0.6 %shard_map.123.refs_5_.refs_7_ = f32[2,4,144,256]{3,2,1,0:T(8,128)S(1)} custom-call(f32[2,6,144,144]{3,2,1,0:T(8,128)S(1)} %bitcast.7), custom_call_target="tpu_custom_call" | custom-call | flops 1000000000 | tf_op jit(solution)/shard_map/pallas_call | solution.py:350
  12.1 0.0 collective-permute-done.refs_1_
  12.1 0.3 copy-done
  12.4 0.1 copy-done.2
  12.5 0.0 copy-done.3
  12.5 0.1 copy-done.5
  12.6 0.1 copy-done.6
  12.7 0.0 copy-done.9
  12.7 1.7 %shard_map.124 = (f32[288,192]{1,0:T(8,128)S(1)}, f32[288,128]{1,0:T(8,128)S(1)}, bf16[288,192]{1,0:T(8,128)(2,1)S(1)}, bf16[2,256,192]{2,1,0:T(8,128)(2,1)S(1)}...) custom-call(bf16[2,144,384]{2,1,0:T(8,128)(2,1)S(1)} %copy-done.5, ...), custom_call_target="tpu_custom_call" | custom-call | flops 1000000000 | tf_op jit(solution)/shard_map/pallas_call | solution.py:350
  14.4 0.0 copy-start.14
  14.4 0.7 %copy-done.14 = f32[288,192]{1,0:T(8,128)} copy-done((f32[288,192]{1,0:T(8,128)}, f32[288,192]{1,0:T(8,128)S(1)}, u32[]{:S(2)}) %copy-start.14) | copy-done | bytes 221208
  15.2 0.7 %copy-done.20 = f32[288,128]{1,0:T(8,128)} copy-done((f32[288,128]{1,0:T(8,128)}, f32[288,128]{1,0:T(8,128)S(1)}, u32[]{:S(2)}) %copy-start.20) | copy-done | bytes 147480
  15.8 0.7 %copy-done.22 = bf16[288,192]{1,0:T(8,128)(2,1)} copy-done((bf16[288,192]{1,0:T(8,128)(2,1)}, bf16[288,192]{1,0:T(8,128)(2,1)S(1)}, u32[]{:S(2)}) %copy-start.22) | copy-done | bytes 110616
  16.5 0.0 collective-permute-done.1.refs_2_
  16.5 0.0 collective-permute-done.2.refs_3_
  16.5 0.0 copy-done.8
  16.5 2.6 %shard_map.125 = (f32[288,192]{1,0:T(8,128)S(1)}, f32[288,128]{1,0:T(8,128)S(1)}, bf16[288,192]{1,0:T(8,128)(2,1)S(1)}, bf16[2,256,192]{2,1,0:T(8,128)(2,1)S(1)}...) custom-call(bf16[2,144,384]{2,1,0:T(8,128)(2,1)S(1)} %copy-done.5, ...), custom_call_target="tpu_custom_call" | custom-call | flops 1000000000 | tf_op jit(solution)/shard_map/pallas_call | solution.py:350
  19.2 0.0 copy-done.10
  19.2 0.0 copy-done.12
  19.2 0.0 copy-done.16
  19.2 0.0 copy-done.18
  19.2 0.0 copy-start.1
  19.2 3.6 %all-to-all-start = ((bf16[4,2,144,256]{3,2,1,0:T(8,128)(2,1)}), bf16[4,2,144,256]{3,2,1,0:T(8,128)(2,1)S(1)}, u32[]{:S(2)}, u32[]{:S(2)}) async-start(bf16[4,2,144,256]{3,2,1,0:T(8,128)(2,1)} %get-tuple-element.55), calls=%async_computation | async-start | bytes 1179648 | tf_op jit(solution)/shard_map/all_to_all | solution.py:426
  22.8 0.0 copy-done.1
  22.8 0.0 copy-start.7
  22.8 0.0 copy-start.11
  22.8 0.0 copy-start.13
  22.9 0.0 copy-start.15
  22.9 0.0 copy-start.17
  22.9 2.3 %shard_map.126 = (bf16[2,144,192]{2,1,0:T(8,128)(2,1)S(1)}, bf16[2,144,192]{2,1,0:T(8,128)(2,1)S(1)}, bf16[2,48,192]{2,1,0:T(8,128)(2,1)}, bf16[2,48,192]{2,1,0:T(8,128)(2,1)S(1)}) custom-call(f32[288,192]{1,0:T(8,128)S(1)} %get-tuple-element.42.refs_0_, f32[288,128]{1,0:T(8,128)S(1)} %get-tuple-element.43.refs_1_, ...), custom_call_target="tpu_custom_call" | custom-call | tf_op jit(solution)/shard_map/pallas_call | solution.py:350
  25.2 0.0 copy-done.15
  25.2 1.7 %shard_map.127 = (bf16[2,144,192]{2,1,0:T(8,128)(2,1)S(1)}, bf16[144,384]{1,0:T(8,128)(2,1)S(1)}) custom-call(f32[288,192]{1,0:T(8,128)S(1)} %copy-done.15, f32[288,128]{1,0:T(8,128)S(1)} %copy-done.21, bf16[288,192]{1,0:T(8,128)(2,1)S(1)} %copy-done.23, bf16[2,256,192]{2,1,0:T(8,128)(2,1)S(1)} %copy-done.17, bf16[2,256,192]{2,1,0:T(8,128)(2,1)S(1)} %copy-done.19, ...), custom_call_target="tpu_custom_call" | custom-call | flops 1000000000 | tf_op jit(solution)/shard_map/pallas_call | solution.py:350
  27.0 0.3 collective-permute-start.3
  27.3 1.7 %collective-permute-start.4 = (bf16[2,48,192]{2,1,0:T(8,128)(2,1)}, bf16[2,48,192]{2,1,0:T(8,128)(2,1)S(1)}, u32[]{:S(2)}, u32[]{:S(2)}) collective-permute-start(bf16[2,48,192]{2,1,0:T(8,128)(2,1)} %get-tuple-element.53), channel_id=1, source_target_pairs={{0,1},{1,2},{2,3},{3,0},{4,5},{5,6},{6,7},{7,4},{8,9},{9,10},{10,1... | collective-permute-start | bytes 110600 | tf_op jit(solution)/shard_map/ppermute | solution.py:368
  29.1 0.8 %collective-permute-start.5 = (bf16[2,48,192]{2,1,0:T(8,128)(2,1)S(1)}, bf16[2,48,192]{2,1,0:T(8,128)(2,1)S(1)}, u32[]{:S(2)}, u32[]{:S(2)}) collective-permute-start(bf16[2,48,192]{2,1,0:T(8,128)(2,1)S(1)} %get-tuple-element.54), channel_id=1, source_target_pairs={{0,5},{1,6},{2,7},{3,4},{4,9},{5,10},{6,11},{7,8},{8,13},{9,14},{1... | collective-permute-start | bytes 110600 | tf_op jit(solution)/shard_map/ppermute | solution.py:368
  29.9 2.9 %all-to-all-done.arrived = bf16[4,2,144,256]{3,2,1,0:T(8,128)(2,1)S(1)} async-done(((bf16[4,2,144,256]{3,2,1,0:T(8,128)(2,1)}), bf16[4,2,144,256]{3,2,1,0:T(8,128)(2,1)S(1)}, u32[]{:S(2)}, u32[]{:S(2)}) %all-to-all-start) | async-done | bytes 589856 | tf_op jit(solution)/shard_map/all_to_all | solution.py:426
  32.8 1.0 %shard_map.128 = (f32[432,1,144]{2,1,0:T(1,128)}, f32[8,128]{1,0:T(8,128)S(1)}) custom-call(bf16[4,2,144,256]{3,2,1,0:T(8,128)(2,1)S(1)} %all-to-all-done.arrived), custom_call_target="tpu_custom_call" | custom-call | flops 1000000000 | tf_op jit(solution)/shard_map/pallas_call | solution.py:350
  33.8 0.4 %collective-permute-done.4.right = bf16[2,48,192]{2,1,0:T(8,128)(2,1)S(1)} collective-permute-done((bf16[2,48,192]{2,1,0:T(8,128)(2,1)}, bf16[2,48,192]{2,1,0:T(8,128)(2,1)S(1)}, u32[]{:S(2)}, u32[]{:S(2)}) %collective-permute-start.4) | collective-permute-done | bytes 36896 | tf_op jit(solution)/shard_map/ppermute | solution.py:368
  34.2 2.0 %collective-permute-done.5.corner = bf16[2,48,192]{2,1,0:T(8,128)(2,1)S(1)} collective-permute-done((bf16[2,48,192]{2,1,0:T(8,128)(2,1)S(1)}, bf16[2,48,192]{2,1,0:T(8,128)(2,1)S(1)}, u32[]{:S(2)}, u32[]{:S(2)}) %collective-permute-start.5) | collective-permute-done | bytes 36896 | tf_op jit(solution)/shard_map/ppermute | solution.py:368
  36.2 0.0 collective-permute-done.3.below
  36.2 0.8 %shard_map.129 = bf16[4,6,24,192]{3,2,1,0:T(8,128)(2,1)} custom-call(bf16[2,144,192]{2,1,0:T(8,128)(2,1)S(1)} %get-tuple-element.51.inner, bf16[144,384]{1,0:T(8,128)(2,1)S(1)} %collective-permute-done.3.below, bf16[2,48,192]{2,1,0:T(8,128)(2,1)S(1)} %collective-permute-done.4.right, bf16[2,48,192]{2,1,0:T(8,128)(2,1)S(1)} %collective-permute-done.5.corner, ...), custom_call_target="tpu_custom_call" | custom-call | tf_op jit(solution)/shard_map/pallas_call | solution.py:350
  (22 shorter events, 0.0 us)
Async XLA Ops:
  2.6 9.4 %collective-permute-start = (bf16[2,144,384]{2,1,0:T(8,128)(2,1)}, bf16[2,144,384]{2,1,0:T(8,128)(2,1)S(1)}, u32[]{:S(2)}, u32[]{:S(2)}) collective-permute-start(bf16[2,144,384]{2,1,0:T(8,128)(2,1)} %get-tuple-element.31), channel_id=1, source_target_pairs={{0,28},{1,29},{2,30},{3,31},{4,0},{5,1},{6,2},{7,3},{8,4},{9,5},{1... | collective-permute-start | bytes 663560 | tf_op jit(solution)/shard_map/ppermute | solution.py:368
  7.2 9.3 %collective-permute-start.1 = (bf16[2,48,384]{2,1,0:T(8,128)(2,1)}, bf16[2,48,384]{2,1,0:T(8,128)(2,1)S(1)}, u32[]{:S(2)}, u32[]{:S(2)}) collective-permute-start(bf16[2,48,384]{2,1,0:T(8,128)(2,1)} %get-tuple-element.39), channel_id=1, source_target_pairs={{0,3},{1,0},{2,1},{3,2},{4,7},{5,4},{6,5},{7,6},{8,11},{9,8},{10,9... | collective-permute-start | bytes 221192 | tf_op jit(solution)/shard_map/ppermute | solution.py:368
  9.6 6.9 %collective-permute-start.2 = (bf16[2,48,384]{2,1,0:T(8,128)(2,1)}, bf16[2,48,384]{2,1,0:T(8,128)(2,1)S(1)}, u32[]{:S(2)}, u32[]{:S(2)}) collective-permute-start(bf16[2,48,384]{2,1,0:T(8,128)(2,1)} %get-tuple-element.40), channel_id=1, source_target_pairs={{0,31},{1,28},{2,29},{3,30},{4,3},{5,0},{6,1},{7,2},{8,7},{9,4},{1... | collective-permute-start | bytes 221192 | tf_op jit(solution)/shard_map/ppermute | solution.py:368
  10.0 1.5 %copy-start.4 = (f32[2,1,6,144,144]{4,3,2,1,0:T(8,128)S(1)}, f32[2,1,6,144,144]{4,3,2,1,0:T(8,128)}, u32[]{:S(2)}) copy-start(f32[2,1,6,144,144]{4,3,2,1,0:T(8,128)} %param.16) | copy-start | bytes 2985988
  11.4 0.9 %copy-start = (bf16[192,576]{1,0:T(8,128)(2,1)S(1)}, bf16[192,576]{1,0:T(8,128)(2,1)}, u32[]{:S(2)}) copy-start(bf16[192,576]{1,0:T(8,128)(2,1)} %refs_8_.4) | copy-start | bytes 663556
  11.4 1.0 %copy-start.2 = (bf16[4,64,144]{2,1,0:T(8,128)(2,1)S(1)}, bf16[4,64,144]{2,1,0:T(8,128)(2,1)}, u32[]{:S(2)}) copy-start(bf16[4,64,144]{2,1,0:T(8,128)(2,1)} %constant.10.clone.refs_7_.refs_9_.refs_10_) | copy-start | bytes 221188
  11.5 1.0 %copy-start.3 = (f32[192]{0:T(256)S(1)}, f32[192]{0:T(256)}, u32[]{:S(2)}) copy-start(f32[192]{0:T(256)} %param.13) | copy-start | bytes 2308
  11.5 1.1 %copy-start.5 = (bf16[2,144,384]{2,1,0:T(8,128)(2,1)S(1)}, bf16[2,144,384]{2,1,0:T(8,128)(2,1)}, u32[]{:S(2)}) copy-start(bf16[2,144,384]{2,1,0:T(8,128)(2,1)} %get-tuple-element.30.refs_0_) | copy-start | bytes 663556
  11.5 1.2 %copy-start.6 = (bf16[192,192]{1,0:T(8,128)(2,1)S(1)}, bf16[192,192]{1,0:T(8,128)(2,1)}, u32[]{:S(2)}) copy-start(bf16[192,192]{1,0:T(8,128)(2,1)} %refs_6_.2) | copy-start | bytes 221188
  11.5 1.2 %copy-start.9 = (bf16[144,288]{1,0:T(8,128)(2,1)S(1)}, bf16[144,288]{1,0:T(8,128)(2,1)}, u32[]{:S(2)}) copy-start(bf16[144,288]{1,0:T(8,128)(2,1)} %constant.11.clone.refs_6_) | copy-start | bytes 248836
  12.7 3.8 %copy-start.8 = (bf16[144,384]{1,0:T(8,128)(2,1)S(1)}, bf16[144,384]{1,0:T(8,128)(2,1)}, u32[]{:S(2)}) copy-start(bf16[144,384]{1,0:T(8,128)(2,1)} %constant.12.clone.refs_8_) | copy-start | bytes 331780
  14.4 0.7 %copy-start.14 = (f32[288,192]{1,0:T(8,128)}, f32[288,192]{1,0:T(8,128)S(1)}, u32[]{:S(2)}) copy-start(f32[288,192]{1,0:T(8,128)S(1)} %get-tuple-element.32.refs_0_) | copy-start | bytes 663556
  15.2 0.7 %copy-start.20 = (f32[288,128]{1,0:T(8,128)}, f32[288,128]{1,0:T(8,128)S(1)}, u32[]{:S(2)}) copy-start(f32[288,128]{1,0:T(8,128)S(1)} %get-tuple-element.33.refs_1_) | copy-start | bytes 442372
  15.8 0.7 %copy-start.22 = (bf16[288,192]{1,0:T(8,128)(2,1)}, bf16[288,192]{1,0:T(8,128)(2,1)S(1)}, u32[]{:S(2)}) copy-start(bf16[288,192]{1,0:T(8,128)(2,1)S(1)} %get-tuple-element.34.refs_2_) | copy-start | bytes 331780
  16.5 2.7 %copy-start.10 = (bf16[2,144,1024]{2,1,0:T(8,128)(2,1)}, bf16[2,144,1024]{2,1,0:T(8,128)(2,1)S(1)}, u32[]{:S(2)}) copy-start(bf16[2,144,1024]{2,1,0:T(8,128)(2,1)S(1)} %get-tuple-element.37.refs_5_) | copy-start | bytes 1769476
  16.5 2.7 %copy-start.12 = (bf16[2,144,1024]{2,1,0:T(8,128)(2,1)}, bf16[2,144,1024]{2,1,0:T(8,128)(2,1)S(1)}, u32[]{:S(2)}) copy-start(bf16[2,144,1024]{2,1,0:T(8,128)(2,1)S(1)} %get-tuple-element.38.refs_6_) | copy-start | bytes 1769476
  16.5 2.7 %copy-start.16 = (bf16[2,256,192]{2,1,0:T(8,128)(2,1)}, bf16[2,256,192]{2,1,0:T(8,128)(2,1)S(1)}, u32[]{:S(2)}) copy-start(bf16[2,256,192]{2,1,0:T(8,128)(2,1)S(1)} %get-tuple-element.35.refs_3_) | copy-start | bytes 589828
  16.5 2.7 %copy-start.18 = (bf16[2,256,192]{2,1,0:T(8,128)(2,1)}, bf16[2,256,192]{2,1,0:T(8,128)(2,1)S(1)}, u32[]{:S(2)}) copy-start(bf16[2,256,192]{2,1,0:T(8,128)(2,1)S(1)} %get-tuple-element.36.refs_4_) | copy-start | bytes 589828
  19.2 3.6 %copy-start.1 = (bf16[384,144]{1,0:T(8,128)(2,1)S(1)}, bf16[384,144]{1,0:T(8,128)(2,1)}, u32[]{:S(2)}) copy-start(bf16[384,144]{1,0:T(8,128)(2,1)} %constant.13.clone.refs_9_) | copy-start | bytes 331780
  19.2 13.6 %all-to-all-start = ((bf16[4,2,144,256]{3,2,1,0:T(8,128)(2,1)}), bf16[4,2,144,256]{3,2,1,0:T(8,128)(2,1)S(1)}, u32[]{:S(2)}, u32[]{:S(2)}) async-start(bf16[4,2,144,256]{3,2,1,0:T(8,128)(2,1)} %get-tuple-element.55), calls=%async_computation | async-start | bytes 1179648 | tf_op jit(solution)/shard_map/all_to_all | solution.py:426
  22.8 2.4 %copy-start.7 = (bf16[288,144]{1,0:T(8,128)(2,1)S(1)}, bf16[288,144]{1,0:T(8,128)(2,1)}, u32[]{:S(2)}) copy-start(bf16[288,144]{1,0:T(8,128)(2,1)} %constant.14.clone.refs_9_) | copy-start | bytes 248836
  22.8 2.4 %copy-start.11 = (bf16[2,144,1024]{2,1,0:T(8,128)(2,1)S(1)}, bf16[2,144,1024]{2,1,0:T(8,128)(2,1)}, u32[]{:S(2)}) copy-start(bf16[2,144,1024]{2,1,0:T(8,128)(2,1)} %copy-done.10) | copy-start | bytes 1769476
  22.8 2.4 %copy-start.13 = (bf16[2,144,1024]{2,1,0:T(8,128)(2,1)S(1)}, bf16[2,144,1024]{2,1,0:T(8,128)(2,1)}, u32[]{:S(2)}) copy-start(bf16[2,144,1024]{2,1,0:T(8,128)(2,1)} %copy-done.12) | copy-start | bytes 1769476
  22.9 2.3 %copy-start.15 = (f32[288,192]{1,0:T(8,128)S(1)}, f32[288,192]{1,0:T(8,128)}, u32[]{:S(2)}) copy-start(f32[288,192]{1,0:T(8,128)} %copy-done.14) | copy-start | bytes 663556
  22.9 2.3 %copy-start.17 = (bf16[2,256,192]{2,1,0:T(8,128)(2,1)S(1)}, bf16[2,256,192]{2,1,0:T(8,128)(2,1)}, u32[]{:S(2)}) copy-start(bf16[2,256,192]{2,1,0:T(8,128)(2,1)} %copy-done.16) | copy-start | bytes 589828
  22.9 2.3 %copy-start.19 = (bf16[2,256,192]{2,1,0:T(8,128)(2,1)S(1)}, bf16[2,256,192]{2,1,0:T(8,128)(2,1)}, u32[]{:S(2)}) copy-start(bf16[2,256,192]{2,1,0:T(8,128)(2,1)} %copy-done.18) | copy-start | bytes 589828
  22.9 2.3 %copy-start.21 = (f32[288,128]{1,0:T(8,128)S(1)}, f32[288,128]{1,0:T(8,128)}, u32[]{:S(2)}) copy-start(f32[288,128]{1,0:T(8,128)} %copy-done.20) | copy-start | bytes 442372
  22.9 2.3 %copy-start.23 = (bf16[288,192]{1,0:T(8,128)(2,1)S(1)}, bf16[288,192]{1,0:T(8,128)(2,1)}, u32[]{:S(2)}) copy-start(bf16[288,192]{1,0:T(8,128)(2,1)} %copy-done.22) | copy-start | bytes 331780
  27.0 9.2 %collective-permute-start.3 = (bf16[144,384]{1,0:T(8,128)(2,1)S(1)}, bf16[144,384]{1,0:T(8,128)(2,1)S(1)}, u32[]{:S(2)}, u32[]{:S(2)}) collective-permute-start(bf16[144,384]{1,0:T(8,128)(2,1)S(1)} %get-tuple-element.52), channel_id=1, source_target_pairs={{0,4},{1,5},{2,6},{3,7},{4,8},{5,9},{6,10},{7,11},{8,12},{9,13},{1... | collective-permute-start | bytes 331784 | tf_op jit(solution)/shard_map/ppermute | solution.py:368
  27.3 6.9 %collective-permute-start.4 = (bf16[2,48,192]{2,1,0:T(8,128)(2,1)}, bf16[2,48,192]{2,1,0:T(8,128)(2,1)S(1)}, u32[]{:S(2)}, u32[]{:S(2)}) collective-permute-start(bf16[2,48,192]{2,1,0:T(8,128)(2,1)} %get-tuple-element.53), channel_id=1, source_target_pairs={{0,1},{1,2},{2,3},{3,0},{4,5},{5,6},{6,7},{7,4},{8,9},{9,10},{10,1... | collective-permute-start | bytes 110600 | tf_op jit(solution)/shard_map/ppermute | solution.py:368
  29.1 7.1 %collective-permute-start.5 = (bf16[2,48,192]{2,1,0:T(8,128)(2,1)S(1)}, bf16[2,48,192]{2,1,0:T(8,128)(2,1)S(1)}, u32[]{:S(2)}, u32[]{:S(2)}) collective-permute-start(bf16[2,48,192]{2,1,0:T(8,128)(2,1)S(1)} %get-tuple-element.54), channel_id=1, source_target_pairs={{0,5},{1,6},{2,7},{3,4},{4,9},{5,10},{6,11},{7,8},{8,13},{9,14},{1... | collective-permute-start | bytes 110600 | tf_op jit(solution)/shard_map/ppermute | solution.py:368

commit v2 on v0

--- a/solution.py
+++ b/solution.py
@@ -99,17 +99,12 @@
     return table
 
 
-def send_kernel(tok, cot, inner, below, right, corner):
-    levels = tok.shape[0]
-
-    def packed(level, row):
-        t, g = tok[level, row].astype(F32), cot[level, row].astype(F32)
-        return jnp.concatenate([t[:, :LANES], g[:, :LANES], t[:, LANES:], g[:, LANES:]], axis=1)
-
+def send_kernel(both, inner, below, right, corner):
+    levels = both.shape[0]
     for a in range(levels // WZ):
         at = [(a * WZ + WZ // 2 + z) % levels for z in range(WZ)]
         for whole, side, base in ((below, corner, 0), (inner, right, HALF_ROWS)):
-            rows = [packed(level, base + row) for level in at for row in range(HALF_ROWS)]
+            rows = [both[level, base + row].astype(F32) for level in at for row in range(HALF_ROWS)]
             whole[a] = jnp.concatenate(rows, axis=0).astype(BF16)
             side[a] = jnp.concatenate([row[:SIDE] for row in rows], axis=0).astype(BF16)
 
@@ -142,7 +137,8 @@
                 rows.append(jnp.zeros((spare, WT), F32))
             turned = jnp.transpose(jnp.concatenate(rows, axis=0)) * LOG2E
             allowed = key_labels == labels(chunks.columns(j), window)
-            bias_t[window, lax.rem(j - me + parts, parts)] = jnp.where(allowed, turned, -1e30)
+            slot = me ^ j if parts & (parts - 1) == 0 else lax.rem(j - me + parts, parts)
+            bias_t[window, slot] = jnp.where(allowed, turned, -1e30)
 
 
 def head_masks(chunks, channels):
@@ -176,9 +172,13 @@
     return [inproj[:, part * channels : (part + 1) * channels] for part in range(3)]
 
 
+def partner(me, d, parts):
+    return me ^ d if parts & (parts - 1) == 0 else (me + d) % parts
+
+
 def rolled(ref, parts):
     me = lax.axis_index("lon")
-    return jnp.concatenate([ref[lax.rem(me + d, parts)] for d in range(parts)], axis=0)
+    return jnp.concatenate([ref[partner(me, d, parts)] for d in range(parts)], axis=0)
 
 
 def scores_kernel(chunks, near, first, last, *refs):
@@ -191,20 +191,20 @@
     standard_out, scale_out, keys_out, query_out, up_out, p_out, ds_out, *totals = refs
     parts, width = chunks.parts, chunks.width
     channels = outproj.shape[0]
-    spare = channels - LANES
     scaling = (channels // chunks.heads) ** (-0.5)
     lanes, rest_mask = head_masks(chunks, channels)
     lanes = [mask.astype(F32).astype(BF16) for mask in lanes]
     rest_mask = rest_mask.astype(BF16) if chunks.rest else None
     choose = rolled(queries, parts)
     level_windows = pieces[0].shape[0]
-    ts, gs = [], []
+    tile = channels // LANES * LANES
+    from_tile = jnp.concatenate([jnp.zeros((channels, channels - tile), BF16), outproj[...]], axis=1)
+    ts, us = [], []
     for a in range(level_windows):
         moved = dot(perm[...], jnp.concatenate([piece[a] for piece in pieces], axis=0))
-        ts.append(jnp.concatenate([moved[:, :LANES], moved[:, 2 * LANES : 2 * LANES + spare]], axis=1))
-        gs.append(jnp.concatenate([moved[:, LANES : 2 * LANES], moved[:, 2 * LANES + spare :]], axis=1))
+        ts.append(moved[:, :channels])
+        us.append(dot_nt(moved[:, tile:].astype(BF16), from_tile).astype(BF16))
     t = jnp.concatenate(ts, axis=0)
-    g = jnp.concatenate(gs, axis=0).astype(BF16)
     centred = t - jnp.mean(t, axis=-1, keepdims=True)
     inverse_rms = lax.rsqrt(jnp.mean(centred * centred, axis=-1, keepdims=True) + epsilon)
     standard = centred * inverse_rms
@@ -214,12 +214,11 @@
     q = dot(normed, weights[0]).astype(BF16)
     k = dot(normed, weights[1]).astype(BF16)
     v = dot(normed, weights[2]).astype(BF16)
-    u = dot_nt(g, outproj[...]).astype(BF16)
     keys_out[...] = k
     for a in range(level_windows):
         cut = slice(a * WT, (a + 1) * WT)
         query = dot(choose, q[cut]).astype(BF16)
-        up = dot(choose, u[cut]).astype(BF16)
+        up = dot(choose, us[a]).astype(BF16)
         query_out[a] = query
         up_out[a] = up
         for d in range(parts):
@@ -314,8 +313,7 @@
     below[...] = jnp.concatenate(packed, axis=1).astype(BF16)
 
 
-def join_kernel(inner, below, grad_input, joined):
-    joined[...] = jnp.zeros(joined.shape, F32)
+def join_kernel(inner, below, after, grad_input):
     levels, _, cols, channels = grad_input.shape
     level_windows = levels // WZ
     whole = below[...].astype(F32)
@@ -333,8 +331,9 @@
                 grad_input[level, HALF_ROWS + row] = high[at].astype(BF16)
 
 
-def bias_kernel(chunks, joined, *refs):
-    arrived, bias_grad = refs[:-1], refs[-1]
+def bias_kernel(chunks, *refs):
+    *arrived, bias_grad, after = refs
+    after[...] = jnp.zeros(after.shape, F32)
     main, rest, heads = chunks.main, chunks.rest, chunks.heads
     for a in range(arrived[0].shape[0]):
         total = arrived[0][a].astype(F32)
@@ -390,7 +389,7 @@
     inner, below, right, corner = call(
         send_kernel,
         [struct((level_windows, size, 2 * channels), BF16) for size in (half, half, side, side)],
-        (tokens, cotangent),
+        (jnp.concatenate([tokens, cotangent], axis=-1),),
     )
     below = shift(below, -1, 0)
     right = shift(right, 0, -1)
@@ -428,7 +427,10 @@
         )
         per_window.append(results[:7])
         total = results[7:]
-    arrived = [total[0]] + [shift(total[d], 0, d) for d in range(1, lon_count)]
+    arrived = [total[0]]
+    for d in range(1, lon_count):
+        pairs = [(i, partner(i, d, lon_count)) for i in range(lon_count)]
+        arrived.append(lax.ppermute(total[d], "lon", pairs))
     grads = []
     for c in reversed(range(windows)):
         last = c == windows - 1
@@ -450,14 +452,13 @@
         (*grads, left, jnp.asarray(side_table.T, BF16)),
     )
     above = shift(g_below, 1, 0)
-    grad_input, joined = call(
-        join_kernel, [struct(tokens.shape, BF16), struct((8, LANES), F32)], (g_inner, above)
-    )
-    (bias_grad,) = call(
+    bias_grad, after = call(
         functools.partial(bias_kernel, chunks),
-        [struct((level_windows * heads * chunks.size, 1, WT), F32)],
-        (joined, *arrived),
-    )
+        [struct((level_windows * heads * chunks.size, 1, WT), F32), struct((8, LANES), F32)],
+        arrived,
+        flops=10**9,
+    )
+    (grad_input,) = call(join_kernel, [struct(tokens.shape, BF16)], (g_inner, above, after))
     bias_grad = bias_grad.reshape(level_windows, heads, chunks.size, 1, WT)
     return grad_input, jnp.transpose(bias_grad, (0, 3, 1, 2, 4))
 

time: 33 us -> 33.8 us (1.024)
  local copies, waits for them, and re-layouts: 3.96 us -> 2.04 us
  waiting for transfers between devices: 5.98 us -> 7.59 us
  other arithmetic: 0 us -> 1.21 us
    ppermute x0 -> x3, starting transfers between devices: none -> 3.55 us  [local(): arrived.append(lax.ppermute(total[d], 'lon', pairs))]
    ppermute x8 -> x5, starting transfers between devices: 12.4 us -> 8.95 us  [shift(): return lax.ppermute(value, ('lat', 'lon'), pairs)]
    unnamed x24 -> x20, local copies, waits for them, and re-layouts: 3.96 us -> 2.04 us
    concatenate x0 -> x1, other arithmetic: none -> 1.21 us  [local(): jnp.concatenate([tokens, cotangent], axis=-1)]
    ppermute x8 -> x5, waiting for transfers between devices: 5.98 us -> 6.79 us  [shift(): return lax.ppermute(value, ('lat', 'lon'), pairs)]
    ppermute x0 -> x3, waiting for transfers between devices: none -> 0.8 us  [local(): arrived.append(lax.ppermute(total[d], 'lon', pairs))]
  transfers between devices with their start and end apart: 8 -> 8, of which waited for: 1 -> 3; matrix products, arithmetic and copies ran while one was open for 0% -> 0% of each run, Pallas kernels for 15% -> 21%
where the time goes in v2:
time: 33.8 us; the launch traced here: 33.6 us
  starting transfers between devices  12.5 us (37%)
  Pallas kernels  9.55 us (28%)
  waiting for transfers between devices  7.59 us (22%)
  local copies, waits for them, and re-layouts  2.04 us (6%)
  other arithmetic  1.21 us (4%)
  between operations  0.75 us (2%)
    pallas_call x9, Pallas kernels, call(): pl.pallas_call(kernel, out_shape=outs, in_specs=vmem(len(args)), out_spec...  9.55 us
    ppermute x5, starting transfers between devices, shift(): return lax.ppermute(value, ('lat', 'lon'), pairs)  8.95 us
    ppermute x5, waiting for transfers between devices, shift(): return lax.ppermute(value, ('lat', 'lon'), pairs)  6.79 us
    ppermute x3, starting transfers between devices, local(): arrived.append(lax.ppermute(total[d], 'lon', pairs))  3.55 us
    unnamed x20, local copies, waits for them, and re-layouts  2.04 us
    concatenate x1, other arithmetic, local(): jnp.concatenate([tokens, cotangent], axis=-1)  1.21 us
    ppermute x3, waiting for transfers between devices, local(): arrived.append(lax.ppermute(total[d], 'lon', pairs))  0.8 us
  transfers between devices with their start and end apart: 8, of which 3 were waited for; matrix products, arithmetic and copies ran while one was open for 0% of the time, Pallas kernels for 21%

profile of v2, /device:TPU:0, one launch (start us, length us, event | category | flops | bytes accessed | tf_op | source)
XLA Modules:
  0.0 33.6 jit_solution(16549274497676474936)
XLA Ops:
  0.6 1.2 %pad_maximum_fusion.both = bf16[4,6,24,384]{3,2,1,0:T(8,128)(2,1)S(1)} fusion(bf16[4,6,24,192]{3,2,1,0:T(8,128)(2,1)} %param.13, bf16[4,6,24,192]{3,2,1,0:T(8,128)(2,1)} %param.12), kind=kLoop, calls=%fused_computation | loop fusion | flops 884736 | bytes 884736 | tf_op jit(solution)/shard_map/concatenate | solution.py:392
  1.8 0.1 shard_map.131
  1.9 4.5 %collective-permute-start = (bf16[2,144,384]{2,1,0:T(8,128)(2,1)S(1)}, bf16[2,144,384]{2,1,0:T(8,128)(2,1)S(1)}, u32[]{:S(2)}, u32[]{:S(2)}) collective-permute-start(bf16[2,144,384]{2,1,0:T(8,128)(2,1)S(1)} %get-tuple-element.35), channel_id=1, source_target_pairs={{0,28},{1,29},{2,30},{3,31},{4,0},{5,1},{6,2},{7,3},{8,4},{9,5},{1... | collective-permute-start | bytes 663560 | tf_op jit(solution)/shard_map/ppermute | solution.py:374
  6.4 2.4 %collective-permute-start.1 = (bf16[2,48,384]{2,1,0:T(8,128)(2,1)S(1)}, bf16[2,48,384]{2,1,0:T(8,128)(2,1)S(1)}, u32[]{:S(2)}, u32[]{:S(2)}) collective-permute-start(bf16[2,48,384]{2,1,0:T(8,128)(2,1)S(1)} %get-tuple-element.43), channel_id=1, source_target_pairs={{0,3},{1,0},{2,1},{3,2},{4,7},{5,4},{6,5},{7,6},{8,11},{9,8},{10,9... | collective-permute-start | bytes 221192 | tf_op jit(solution)/shard_map/ppermute | solution.py:374
  8.9 0.4 %collective-permute-start.2 = (bf16[2,48,384]{2,1,0:T(8,128)(2,1)S(1)}, bf16[2,48,384]{2,1,0:T(8,128)(2,1)S(1)}, u32[]{:S(2)}, u32[]{:S(2)}) collective-permute-start(bf16[2,48,384]{2,1,0:T(8,128)(2,1)S(1)} %get-tuple-element.44), channel_id=1, source_target_pairs={{0,31},{1,28},{2,29},{3,30},{4,3},{5,0},{6,1},{7,2},{8,7},{9,4},{1... | collective-permute-start | bytes 221192 | tf_op jit(solution)/shard_map/ppermute | solution.py:374
  9.3 0.0 copy-start.6
  9.3 1.5 %copy-done.6 = f32[2,1,6,144,144]{4,3,2,1,0:T(8,128)S(1)} copy-done((f32[2,1,6,144,144]{4,3,2,1,0:T(8,128)S(1)}, f32[2,1,6,144,144]{4,3,2,1,0:T(8,128)}, u32[]{:S(2)}) %copy-start.6) | copy-done | bytes 995352
  10.7 0.0 copy-start
  10.7 0.0 copy-start.1
  10.7 0.0 copy-start.5
  10.7 0.0 copy-start.7
  10.7 0.0 copy-start.9
  10.8 0.6 %shard_map.132.refs_5_.refs_7_ = f32[2,4,144,256]{3,2,1,0:T(8,128)S(1)} custom-call(f32[2,6,144,144]{3,2,1,0:T(8,128)S(1)} %bitcast.7), custom_call_target="tpu_custom_call" | custom-call | flops 1000000000 | tf_op jit(solution)/shard_map/pallas_call | solution.py:357
  11.3 0.0 collective-permute-done.refs_1_
  11.3 0.3 copy-done
  11.7 0.1 copy-done.1
  11.8 0.0 copy-done.5
  11.8 0.1 copy-done.7
  11.8 0.1 copy-done.9
  11.9 0.0 copy-start.8
  11.9 1.7 %shard_map.133 = (f32[288,192]{1,0:T(8,128)S(1)}, f32[288,128]{1,0:T(8,128)S(1)}, bf16[288,192]{1,0:T(8,128)(2,1)S(1)}, bf16[2,256,192]{2,1,0:T(8,128)(2,1)S(1)}...) custom-call(bf16[2,144,384]{2,1,0:T(8,128)(2,1)S(1)} %get-tuple-elem, ...), custom_call_target="tpu_custom_call" | custom-call | flops 1000000000 | tf_op jit(solution)/shard_map/pallas_call | solution.py:357
  13.6 0.0 collective-permute-done.1.refs_2_
  13.6 0.0 collective-permute-done.2.refs_3_
  13.7 0.0 copy-done.8
  13.7 0.0 copy-start.2
  13.7 1.8 %shard_map.134 = (f32[288,192]{1,0:T(8,128)S(1)}, f32[288,128]{1,0:T(8,128)S(1)}, bf16[288,192]{1,0:T(8,128)(2,1)S(1)}, bf16[2,256,192]{2,1,0:T(8,128)(2,1)S(1)}...) custom-call(bf16[2,144,384]{2,1,0:T(8,128)(2,1)S(1)} %get-tuple-elem, ...), custom_call_target="tpu_custom_call" | custom-call | flops 1000000000 | tf_op jit(solution)/shard_map/pallas_call | solution.py:357
  15.5 1.6 %collective-permute-start.5 = (bf16[2,144,256]{2,1,0:T(8,128)(2,1)S(1)}, bf16[2,144,256]{2,1,0:T(8,128)(2,1)S(1)}, u32[]{:S(2)}, u32[]{:S(2)}) collective-permute-start(bf16[2,144,256]{2,1,0:T(8,128)(2,1)S(1)} %get-tuple-element.61), channel_id=1, source_target_pairs={{0,1},{1,0},{2,3},{3,2},{4,5},{5,4},{6,7},{7,6},{8,9},{9,8},{10,11... | collective-permute-start | bytes 442376 | tf_op jit(solution)/shard_map/ppermute | solution.py:433
  17.0 0.5 %collective-permute-start.6 = (bf16[2,144,256]{2,1,0:T(8,128)(2,1)S(1)}, bf16[2,144,256]{2,1,0:T(8,128)(2,1)S(1)}, u32[]{:S(2)}, u32[]{:S(2)}) collective-permute-start(bf16[2,144,256]{2,1,0:T(8,128)(2,1)S(1)} %get-tuple-element.62), channel_id=1, source_target_pairs={{0,2},{1,3},{2,0},{3,1},{4,6},{5,7},{6,4},{7,5},{8,10},{9,11},{10,... | collective-permute-start | bytes 442376 | tf_op jit(solution)/shard_map/ppermute | solution.py:433
  17.5 1.5 %collective-permute-start.7 = (bf16[2,144,256]{2,1,0:T(8,128)(2,1)S(1)}, bf16[2,144,256]{2,1,0:T(8,128)(2,1)S(1)}, u32[]{:S(2)}, u32[]{:S(2)}) collective-permute-start(bf16[2,144,256]{2,1,0:T(8,128)(2,1)S(1)} %get-tuple-element.63), channel_id=1, source_target_pairs={{0,3},{1,2},{2,1},{3,0},{4,7},{5,6},{6,5},{7,4},{8,11},{9,10},{10,... | collective-permute-start | bytes 442376 | tf_op jit(solution)/shard_map/ppermute | solution.py:433
  19.0 0.0 copy-done.2
  19.0 0.0 copy-start.3
  19.0 1.7 %shard_map.135 = (bf16[2,144,192]{2,1,0:T(8,128)(2,1)S(1)}, bf16[2,144,192]{2,1,0:T(8,128)(2,1)S(1)}, bf16[2,80,192]{2,1,0:T(8,128)(2,1)S(1)}) custom-call(f32[288,192]{1,0:T(8,128)S(1)} %get-tuple-element.46.refs_0_, f32[288,128]{1,0:T(8,128)S(1)} %get-tuple-element.47.refs_1_, bf16[288,192]{1,0:T(8,128)(2,1)S(1)} %get-tuple-element.48.refs_2_, ...), custom_call_target="tpu_custom_call" | custom-call | tf_op jit(solution)/shard_map/pallas_call | solution.py:357
  20.7 1.5 %collective-permute-start.3 = (bf16[2,80,192]{2,1,0:T(8,128)(2,1)S(1)}, bf16[2,80,192]{2,1,0:T(8,128)(2,1)S(1)}, u32[]{:S(2)}, u32[]{:S(2)}) collective-permute-start(bf16[2,80,192]{2,1,0:T(8,128)(2,1)S(1)} %get-tuple-element.57), channel_id=1, source_target_pairs={{0,1},{1,2},{2,3},{3,0},{4,5},{5,6},{6,7},{7,4},{8,9},{9,10},{10,1... | collective-permute-start | bytes 184328 | tf_op jit(solution)/shard_map/ppermute | solution.py:374
  22.3 0.0 copy-done.3
  22.3 0.0 copy-start.4
  22.3 1.6 %shard_map.136 = (bf16[2,144,192]{2,1,0:T(8,128)(2,1)S(1)}, bf16[2,144,192]{2,1,0:T(8,128)(2,1)S(1)}) custom-call(f32[288,192]{1,0:T(8,128)S(1)} %get-tuple-element.36.refs_0_, f32[288,128]{1,0:T(8,128)S(1)} %get-tuple-element.37.refs_1_, bf16[288,192]{1,0:T(8,128)(2,1)S(1)} %get-tuple-element.38.refs_2_, ...), custom_call_target="tpu_custom_call" | custom-call | tf_op jit(solution)/shard_map/pallas_call | solution.py:357
  23.9 2.6 %collective-permute-done.3.side = bf16[2,80,192]{2,1,0:T(8,128)(2,1)S(1)} collective-permute-done((bf16[2,80,192]{2,1,0:T(8,128)(2,1)S(1)}, bf16[2,80,192]{2,1,0:T(8,128)(2,1)S(1)}, u32[]{:S(2)}, u32[]{:S(2)}) %collective-permute-start.3) | collective-permute-done | bytes 61472 | tf_op jit(solution)/shard_map/ppermute | solution.py:374
  26.5 0.0 copy-done.4
  26.5 0.3 shard_map.137
  26.8 0.1 collective-permute-start.4
  26.9 0.0 collective-permute-done.5.refs_1_
  26.9 0.8 %collective-permute-done.6.refs_2_ = bf16[2,144,256]{2,1,0:T(8,128)(2,1)S(1)} collective-permute-done((bf16[2,144,256]{2,1,0:T(8,128)(2,1)S(1)}, bf16[2,144,256]{2,1,0:T(8,128)(2,1)S(1)}, u32[]{:S(2)}, u32[]{:S(2)}) %collective-permute-start.6) | collective-permute-done | bytes 147488 | tf_op jit(solution)/shard_map/ppermute | solution.py:433
  27.7 0.0 collective-permute-done.7.refs_3_
  27.7 1.0 %shard_map.138 = (f32[432,1,144]{2,1,0:T(1,128)}, f32[8,128]{1,0:T(8,128)S(1)}) custom-call(bf16[2,144,256]{2,1,0:T(8,128)(2,1)S(1)} %get-tuple-element.60.refs_0_, bf16[2,144,256]{2,1,0:T(8,128)(2,1)S(1)} %collective-permute-done.5.refs_1_, bf16[2,144,256]{2,1,0:T(8,128)(2,1)S(1)} %collective-permute-done.6.refs_2_, ...), custom_call_target="tpu_custom_call" | custom-call | flops 1000000000 | tf_op jit(solution)/shard_map/pallas_call | solution.py:357
  28.7 4.2 %collective-permute-done.4.below = bf16[144,384]{1,0:T(8,128)(2,1)S(1)} collective-permute-done((bf16[144,384]{1,0:T(8,128)(2,1)S(1)}, bf16[144,384]{1,0:T(8,128)(2,1)S(1)}, u32[]{:S(2)}, u32[]{:S(2)}) %collective-permute-start.4) | collective-permute-done | bytes 110624 | tf_op jit(solution)/shard_map/ppermute | solution.py:374
  32.8 0.8 %shard_map.139 = bf16[4,6,24,192]{3,2,1,0:T(8,128)(2,1)} custom-call(bf16[2,144,192]{2,1,0:T(8,128)(2,1)S(1)} %get-tuple-element.58.inner, bf16[144,384]{1,0:T(8,128)(2,1)S(1)} %collective-permute-done.4.below, f32[8,128]{1,0:T(8,128)S(1)} %get-tuple-element.64.after), custom_call_target="tpu_custom_call" | custom-call | tf_op jit(solution)/shard_map/pallas_call | solution.py:357
Async XLA Ops:
  1.9 9.4 %collective-permute-start = (bf16[2,144,384]{2,1,0:T(8,128)(2,1)S(1)}, bf16[2,144,384]{2,1,0:T(8,128)(2,1)S(1)}, u32[]{:S(2)}, u32[]{:S(2)}) collective-permute-start(bf16[2,144,384]{2,1,0:T(8,128)(2,1)S(1)} %get-tuple-element.35), channel_id=1, source_target_pairs={{0,28},{1,29},{2,30},{3,31},{4,0},{5,1},{6,2},{7,3},{8,4},{9,5},{1... | collective-permute-start | bytes 663560 | tf_op jit(solution)/shard_map/ppermute | solution.py:374
  6.4 7.2 %collective-permute-start.1 = (bf16[2,48,384]{2,1,0:T(8,128)(2,1)S(1)}, bf16[2,48,384]{2,1,0:T(8,128)(2,1)S(1)}, u32[]{:S(2)}, u32[]{:S(2)}) collective-permute-start(bf16[2,48,384]{2,1,0:T(8,128)(2,1)S(1)} %get-tuple-element.43), channel_id=1, source_target_pairs={{0,3},{1,0},{2,1},{3,2},{4,7},{5,4},{6,5},{7,6},{8,11},{9,8},{10,9... | collective-permute-start | bytes 221192 | tf_op jit(solution)/shard_map/ppermute | solution.py:374
  8.9 4.8 %collective-permute-start.2 = (bf16[2,48,384]{2,1,0:T(8,128)(2,1)S(1)}, bf16[2,48,384]{2,1,0:T(8,128)(2,1)S(1)}, u32[]{:S(2)}, u32[]{:S(2)}) collective-permute-start(bf16[2,48,384]{2,1,0:T(8,128)(2,1)S(1)} %get-tuple-element.44), channel_id=1, source_target_pairs={{0,31},{1,28},{2,29},{3,30},{4,3},{5,0},{6,1},{7,2},{8,7},{9,4},{1... | collective-permute-start | bytes 221192 | tf_op jit(solution)/shard_map/ppermute | solution.py:374
  9.3 1.5 %copy-start.6 = (f32[2,1,6,144,144]{4,3,2,1,0:T(8,128)S(1)}, f32[2,1,6,144,144]{4,3,2,1,0:T(8,128)}, u32[]{:S(2)}) copy-start(f32[2,1,6,144,144]{4,3,2,1,0:T(8,128)} %param.17) | copy-start | bytes 2985988
  10.7 0.9 %copy-start = (bf16[192,576]{1,0:T(8,128)(2,1)S(1)}, bf16[192,576]{1,0:T(8,128)(2,1)}, u32[]{:S(2)}) copy-start(bf16[192,576]{1,0:T(8,128)(2,1)} %refs_8_.4) | copy-start | bytes 663556
  10.7 1.0 %copy-start.1 = (bf16[4,64,144]{2,1,0:T(8,128)(2,1)S(1)}, bf16[4,64,144]{2,1,0:T(8,128)(2,1)}, u32[]{:S(2)}) copy-start(bf16[4,64,144]{2,1,0:T(8,128)(2,1)} %constant.12.clone.refs_7_.refs_9_.refs_10_) | copy-start | bytes 221188
  10.7 1.0 %copy-start.5 = (f32[192]{0:T(256)S(1)}, f32[192]{0:T(256)}, u32[]{:S(2)}) copy-start(f32[192]{0:T(256)} %param.14) | copy-start | bytes 2308
  10.7 1.1 %copy-start.7 = (bf16[192,192]{1,0:T(8,128)(2,1)S(1)}, bf16[192,192]{1,0:T(8,128)(2,1)}, u32[]{:S(2)}) copy-start(bf16[192,192]{1,0:T(8,128)(2,1)} %refs_6_.2) | copy-start | bytes 221188
  10.7 1.1 %copy-start.9 = (bf16[144,288]{1,0:T(8,128)(2,1)S(1)}, bf16[144,288]{1,0:T(8,128)(2,1)}, u32[]{:S(2)}) copy-start(bf16[144,288]{1,0:T(8,128)(2,1)} %constant.13.clone.refs_6_) | copy-start | bytes 248836
  11.9 1.8 %copy-start.8 = (bf16[144,384]{1,0:T(8,128)(2,1)S(1)}, bf16[144,384]{1,0:T(8,128)(2,1)}, u32[]{:S(2)}) copy-start(bf16[144,384]{1,0:T(8,128)(2,1)} %constant.14.clone.refs_8_) | copy-start | bytes 331780
  13.7 5.4 %copy-start.2 = (bf16[368,144]{1,0:T(8,128)(2,1)S(1)}, bf16[368,144]{1,0:T(8,128)(2,1)}, u32[]{:S(2)}) copy-start(bf16[368,144]{1,0:T(8,128)(2,1)} %constant.15.clone.refs_9_) | copy-start | bytes 317956
  15.5 11.4 %collective-permute-start.5 = (bf16[2,144,256]{2,1,0:T(8,128)(2,1)S(1)}, bf16[2,144,256]{2,1,0:T(8,128)(2,1)S(1)}, u32[]{:S(2)}, u32[]{:S(2)}) collective-permute-start(bf16[2,144,256]{2,1,0:T(8,128)(2,1)S(1)} %get-tuple-element.61), channel_id=1, source_target_pairs={{0,1},{1,0},{2,3},{3,2},{4,5},{5,4},{6,7},{7,6},{8,9},{9,8},{10,11... | collective-permute-start | bytes 442376 | tf_op jit(solution)/shard_map/ppermute | solution.py:433
  17.0 10.7 %collective-permute-start.6 = (bf16[2,144,256]{2,1,0:T(8,128)(2,1)S(1)}, bf16[2,144,256]{2,1,0:T(8,128)(2,1)S(1)}, u32[]{:S(2)}, u32[]{:S(2)}) collective-permute-start(bf16[2,144,256]{2,1,0:T(8,128)(2,1)S(1)} %get-tuple-element.62), channel_id=1, source_target_pairs={{0,2},{1,3},{2,0},{3,1},{4,6},{5,7},{6,4},{7,5},{8,10},{9,11},{10,... | collective-permute-start | bytes 442376 | tf_op jit(solution)/shard_map/ppermute | solution.py:433
  17.5 10.2 %collective-permute-start.7 = (bf16[2,144,256]{2,1,0:T(8,128)(2,1)S(1)}, bf16[2,144,256]{2,1,0:T(8,128)(2,1)S(1)}, u32[]{:S(2)}, u32[]{:S(2)}) collective-permute-start(bf16[2,144,256]{2,1,0:T(8,128)(2,1)S(1)} %get-tuple-element.63), channel_id=1, source_target_pairs={{0,3},{1,2},{2,1},{3,0},{4,7},{5,6},{6,5},{7,4},{8,11},{9,10},{10,... | collective-permute-start | bytes 442376 | tf_op jit(solution)/shard_map/ppermute | solution.py:433
  19.0 3.2 %copy-start.3 = (bf16[288,144]{1,0:T(8,128)(2,1)S(1)}, bf16[288,144]{1,0:T(8,128)(2,1)}, u32[]{:S(2)}) copy-start(bf16[288,144]{1,0:T(8,128)(2,1)} %constant.16.clone.refs_9_) | copy-start | bytes 248836
  20.7 5.8 %collective-permute-start.3 = (bf16[2,80,192]{2,1,0:T(8,128)(2,1)S(1)}, bf16[2,80,192]{2,1,0:T(8,128)(2,1)S(1)}, u32[]{:S(2)}, u32[]{:S(2)}) collective-permute-start(bf16[2,80,192]{2,1,0:T(8,128)(2,1)S(1)} %get-tuple-element.57), channel_id=1, source_target_pairs={{0,1},{1,2},{2,3},{3,0},{4,5},{5,6},{6,7},{7,4},{8,9},{9,10},{10,1... | collective-permute-start | bytes 184328 | tf_op jit(solution)/shard_map/ppermute | solution.py:374
  22.3 4.3 %copy-start.4 = (bf16[288,80]{1,0:T(8,128)(2,1)S(1)}, bf16[288,80]{1,0:T(8,128)(2,1)}, u32[]{:S(2)}) copy-start(bf16[288,80]{1,0:T(8,128)(2,1)} %constant.17.clone.order_t) | copy-start | bytes 138244
  26.8 6.0 %collective-permute-start.4 = (bf16[144,384]{1,0:T(8,128)(2,1)S(1)}, bf16[144,384]{1,0:T(8,128)(2,1)S(1)}, u32[]{:S(2)}, u32[]{:S(2)}) collective-permute-start(bf16[144,384]{1,0:T(8,128)(2,1)S(1)} %get-tuple-element.59), channel_id=1, source_target_pairs={{0,4},{1,5},{2,6},{3,7},{4,8},{5,9},{6,10},{7,11},{8,12},{9,13},{1... | collective-permute-start | bytes 331784 | tf_op jit(solution)/shard_map/ppermute | solution.py:374

commit v3 on v2

--- a/solution.py
+++ b/solution.py
@@ -67,23 +67,11 @@
         return j * self.size + jnp.where(lane < low, main, left)
 
 
-def side_order(cols):
-    part = HALF_ROWS * cols
-    table = np.zeros((round_up(WZ * WH * HALF_COLS, 16), 2 * WZ * part), np.float32)
-    for z in range(WZ):
-        for r in range(WH):
-            low, row = divmod(r, HALF_ROWS)
-            for w in range(HALF_COLS):
-                table[(z * WH + r) * HALF_COLS + w, (low * WZ + z) * part + row * cols + w] = 1.0
-    return table
-
-
-def window_order(cols, c, out):
+def window_order(cols, c):
     last = c == cols // WW - 1
     part, side = HALF_ROWS * cols, HALF_ROWS * SIDE
     near = 2 * WZ * part
-    extra = round_up(WZ * WH * HALF_COLS, 16) if out else 2 * WZ * side
-    table = np.zeros((WT, near + last * extra), np.float32)
+    table = np.zeros((WT, near + last * 2 * WZ * side), np.float32)
     for z in range(WZ):
         for r in range(WH):
             for w in range(WW):
@@ -91,8 +79,6 @@
                 low, row = divmod(r, HALF_ROWS)
                 if col < cols:
                     at = (low * WZ + z) * part + row * cols + col
-                elif out:
-                    at = near + (z * WH + r) * HALF_COLS + col - cols
                 else:
                     at = near + (low * WZ + z) * side + row * SIDE + col - cols
                 table[(z * WH + r) * WW + w, at] = 1.0
@@ -290,30 +276,26 @@
         - standard * jnp.mean(scaled * standard, axis=-1, keepdims=True)
     )
     grad = grad.astype(BF16)
+    lows = []
     for a in range(level_windows):
         spread = dot(perm_t[...], grad[a * WT : (a + 1) * WT])
         base = 0
         for i, out in enumerate(outs):
-            rows = out.shape[1]
+            rows = out.shape[-2]
             part = spread[base : base + rows]
             if not first and i < 2:
                 part += before[i][a].astype(F32)
-            out[a] = part.astype(BF16)
+            if not first and i == 1:
+                lows.append(part)
+            else:
+                out[a] = part.astype(BF16)
             base += rows
-
-
-def merge_kernel(inner_in, below_in, side, order_t, inner, below):
-    half = inner.shape[1]
-    lows = []
-    for a in range(inner.shape[0]):
-        spread = dot(order_t[...], side[a])
-        inner[a] = (inner_in[a].astype(F32) + spread[:half]).astype(BF16)
-        lows.append(below_in[a].astype(F32) + spread[half:])
-    packed = [low[:, :LANES] for low in lows] + [low[:, LANES:] for low in lows]
-    below[...] = jnp.concatenate(packed, axis=1).astype(BF16)
-
-
-def join_kernel(inner, below, after, grad_input):
+    if not first:
+        packed = [low[:, :LANES] for low in lows] + [low[:, LANES:] for low in lows]
+        outs[1][...] = jnp.concatenate(packed, axis=1).astype(BF16)
+
+
+def join_kernel(inner, below, right, corner, after, grad_input):
     levels, _, cols, channels = grad_input.shape
     level_windows = levels // WZ
     whole = below[...].astype(F32)
@@ -322,13 +304,15 @@
         low = jnp.concatenate(
             [whole[:, a * LANES : (a + 1) * LANES], whole[:, rest_at : rest_at + channels - LANES]], axis=1
         )
-        high = inner[a].astype(F32)
+        parts = ((low, corner[a].astype(F32), 0), (inner[a].astype(F32), right[a].astype(F32), HALF_ROWS))
         for z in range(WZ):
             level = (a * WZ + WZ // 2 + z) % levels
             for row in range(HALF_ROWS):
-                at = slice((z * HALF_ROWS + row) * cols, (z * HALF_ROWS + row + 1) * cols)
-                grad_input[level, row] = low[at].astype(BF16)
-                grad_input[level, HALF_ROWS + row] = high[at].astype(BF16)
+                at = z * HALF_ROWS + row
+                for wide, side, base in parts:
+                    first = wide[at * cols : at * cols + SIDE] + side[at * SIDE : (at + 1) * SIDE]
+                    rest = wide[at * cols + SIDE : (at + 1) * cols]
+                    grad_input[level, base + row] = jnp.concatenate([first, rest], axis=0).astype(BF16)
 
 
 def bias_kernel(chunks, *refs):
@@ -383,7 +367,6 @@
     struct = jax.ShapeDtypeStruct
     half, side = WZ * HALF_ROWS * cols, WZ * HALF_ROWS * SIDE
     gain = norm_gain.reshape(1, channels)
-    side_table = side_order(cols)
     queries = jnp.asarray(chunks.queries(), BF16)
 
     inner, below, right, corner = call(
@@ -409,7 +392,7 @@
             sums = [struct((level_windows, WT, chunks.width), BF16)] * lon_count
         else:
             sums = [struct((level_windows, lon_count, WT, chunks.width), F32)]
-        order = jnp.asarray(window_order(cols, c, False), BF16)
+        order = jnp.asarray(window_order(cols, c), BF16)
         results = call(
             functools.partial(scores_kernel, chunks, len(pieces), c == 0, last),
             [
@@ -431,34 +414,27 @@
     for d in range(1, lon_count):
         pairs = [(i, partner(i, d, lon_count)) for i in range(lon_count)]
         arrived.append(lax.ppermute(total[d], "lon", pairs))
+    wide = struct((level_windows, half, channels), BF16)
+    thin = struct((level_windows, side, channels), BF16)
     grads = []
     for c in reversed(range(windows)):
         last = c == windows - 1
-        outs = [struct((level_windows, half, channels), BF16)] * 2
-        if last:
-            outs.append(struct((level_windows, side_table.shape[0], channels), BF16))
-        order = jnp.asarray(window_order(cols, c, True).T, BF16)
+        order = jnp.asarray(window_order(cols, c).T, BF16)
         results = call(
             functools.partial(tokens_kernel, chunks, 2, last),
-            outs,
+            [wide, wide, thin, thin] if last else [wide, struct((half, level_windows * channels), BF16)],
             (*per_window[c], gain, inproj_weight, order, queries, *grads),
         )
         grads = results[:2]
         if last:
-            left = shift(results[2], 0, 1)
-    g_inner, g_below = call(
-        merge_kernel,
-        [struct((level_windows, half, channels), BF16), struct((half, level_windows * channels), BF16)],
-        (*grads, left, jnp.asarray(side_table.T, BF16)),
-    )
-    above = shift(g_below, 1, 0)
+            left, corner = shift(results[2], 0, 1), shift(results[3], 1, 1)
+    above = shift(grads[1], 1, 0)
     bias_grad, after = call(
         functools.partial(bias_kernel, chunks),
         [struct((level_windows * heads * chunks.size, 1, WT), F32), struct((8, LANES), F32)],
         arrived,
-        flops=10**9,
-    )
-    (grad_input,) = call(join_kernel, [struct(tokens.shape, BF16)], (g_inner, above, after))
+    )
+    (grad_input,) = call(join_kernel, [struct(tokens.shape, BF16)], (grads[0], above, left, corner, after))
     bias_grad = bias_grad.reshape(level_windows, heads, chunks.size, 1, WT)
     return grad_input, jnp.transpose(bias_grad, (0, 3, 1, 2, 4))
 

time: 33.8 us -> 32.1 us (0.950)
  waiting for transfers between devices: 7.59 us -> 6.12 us
    ppermute x5 -> x6, waiting for transfers between devices: 6.79 us -> 3.71 us  [shift(): return lax.ppermute(value, ('lat', 'lon'), pairs)]
    ppermute x3, waiting for transfers between devices: 0.8 us -> 2.41 us  [local(): arrived.append(lax.ppermute(total[d], 'lon', pairs))]
    pallas_call x9 -> x8, Pallas kernels: 9.55 us -> 9.33 us  [call(): pl.pallas_call(kernel, out_shape=outs, in_specs=vmem(len(args)), out_spec...]
    unnamed x20 -> x18, local copies, waits for them, and re-layouts: 2.04 us -> 2.04 us
    ppermute x5 -> x6, starting transfers between devices: 8.95 us -> 8.96 us  [shift(): return lax.ppermute(value, ('lat', 'lon'), pairs)]
  transfers between devices with their start and end apart: 8 -> 9, of which waited for: 3 -> 3; matrix products, arithmetic and copies ran while one was open for 0% -> 0% of each run, Pallas kernels for 21% -> 21%
where the time goes in v3:
time: 32.1 us; the launch traced here: 32 us
  starting transfers between devices  12.5 us (39%)
  Pallas kernels  9.33 us (29%)
  waiting for transfers between devices  6.12 us (19%)
  local copies, waits for them, and re-layouts  2.04 us (6%)
  other arithmetic  1.21 us (4%)
  between operations  0.75 us (2%)
    pallas_call x8, Pallas kernels, call(): pl.pallas_call(kernel, out_shape=outs, in_specs=vmem(len(args)), out_spec...  9.33 us
    ppermute x6, starting transfers between devices, shift(): return lax.ppermute(value, ('lat', 'lon'), pairs)  8.96 us
    ppermute x6, waiting for transfers between devices, shift(): return lax.ppermute(value, ('lat', 'lon'), pairs)  3.71 us
    ppermute x3, starting transfers between devices, local(): arrived.append(lax.ppermute(total[d], 'lon', pairs))  3.55 us
    ppermute x3, waiting for transfers between devices, local(): arrived.append(lax.ppermute(total[d], 'lon', pairs))  2.41 us
    unnamed x18, local copies, waits for them, and re-layouts  2.04 us
    concatenate x1, other arithmetic, local(): jnp.concatenate([tokens, cotangent], axis=-1)  1.21 us
  transfers between devices with their start and end apart: 9, of which 3 were waited for; matrix products, arithmetic and copies ran while one was open for 0% of the time, Pallas kernels for 21%

profile of v3, /device:TPU:0, one launch (start us, length us, event | category | flops | bytes accessed | tf_op | source)
XLA Modules:
  0.0 32.0 jit_solution(4429854879088169173)
XLA Ops:
  0.6 1.2 %pad_maximum_fusion.both = bf16[4,6,24,384]{3,2,1,0:T(8,128)(2,1)S(1)} fusion(bf16[4,6,24,192]{3,2,1,0:T(8,128)(2,1)} %param.12, bf16[4,6,24,192]{3,2,1,0:T(8,128)(2,1)} %param.11), kind=kLoop, calls=%fused_computation | loop fusion | flops 884736 | bytes 884736 | tf_op jit(solution)/shard_map/concatenate | solution.py:375
  1.8 0.1 shard_map.122
  1.9 4.5 %collective-permute-start = (bf16[2,144,384]{2,1,0:T(8,128)(2,1)S(1)}, bf16[2,144,384]{2,1,0:T(8,128)(2,1)S(1)}, u32[]{:S(2)}, u32[]{:S(2)}) collective-permute-start(bf16[2,144,384]{2,1,0:T(8,128)(2,1)S(1)} %get-tuple-element.34), channel_id=1, source_target_pairs={{0,28},{1,29},{2,30},{3,31},{4,0},{5,1},{6,2},{7,3},{8,4},{9,5},{1... | collective-permute-start | bytes 663560 | tf_op jit(solution)/shard_map/ppermute | solution.py:358
  6.4 2.4 %collective-permute-start.1 = (bf16[2,48,384]{2,1,0:T(8,128)(2,1)S(1)}, bf16[2,48,384]{2,1,0:T(8,128)(2,1)S(1)}, u32[]{:S(2)}, u32[]{:S(2)}) collective-permute-start(bf16[2,48,384]{2,1,0:T(8,128)(2,1)S(1)} %get-tuple-element.42), channel_id=1, source_target_pairs={{0,3},{1,0},{2,1},{3,2},{4,7},{5,4},{6,5},{7,6},{8,11},{9,8},{10,9... | collective-permute-start | bytes 221192 | tf_op jit(solution)/shard_map/ppermute | solution.py:358
  8.9 0.4 %collective-permute-start.2 = (bf16[2,48,384]{2,1,0:T(8,128)(2,1)S(1)}, bf16[2,48,384]{2,1,0:T(8,128)(2,1)S(1)}, u32[]{:S(2)}, u32[]{:S(2)}) collective-permute-start(bf16[2,48,384]{2,1,0:T(8,128)(2,1)S(1)} %get-tuple-element.43), channel_id=1, source_target_pairs={{0,31},{1,28},{2,29},{3,30},{4,3},{5,0},{6,1},{7,2},{8,7},{9,4},{1... | collective-permute-start | bytes 221192 | tf_op jit(solution)/shard_map/ppermute | solution.py:358
  9.3 0.0 copy-start.5
  9.3 1.5 %copy-done.5 = f32[2,1,6,144,144]{4,3,2,1,0:T(8,128)S(1)} copy-done((f32[2,1,6,144,144]{4,3,2,1,0:T(8,128)S(1)}, f32[2,1,6,144,144]{4,3,2,1,0:T(8,128)}, u32[]{:S(2)}) %copy-start.5) | copy-done | bytes 995352
  10.7 0.0 copy-start
  10.7 0.0 copy-start.1
  10.7 0.0 copy-start.4
  10.7 0.0 copy-start.6
  10.7 0.0 copy-start.8
  10.8 0.6 %shard_map.123.refs_5_.refs_7_ = f32[2,4,144,256]{3,2,1,0:T(8,128)S(1)} custom-call(f32[2,6,144,144]{3,2,1,0:T(8,128)S(1)} %bitcast.7), custom_call_target="tpu_custom_call" | custom-call | flops 1000000000 | tf_op jit(solution)/shard_map/pallas_call | solution.py:341
  11.3 0.0 collective-permute-done.refs_1_
  11.3 0.3 %copy-done = bf16[192,576]{1,0:T(8,128)(2,1)S(1)} copy-done((bf16[192,576]{1,0:T(8,128)(2,1)S(1)}, bf16[192,576]{1,0:T(8,128)(2,1)}, u32[]{:S(2)}) %copy-start) | copy-done | bytes 221208
  11.7 0.1 copy-done.1
  11.8 0.0 copy-done.4
  11.8 0.1 copy-done.6
  11.8 0.1 copy-done.8
  11.9 0.0 copy-start.7
  11.9 1.7 %shard_map.124 = (f32[288,192]{1,0:T(8,128)S(1)}, f32[288,128]{1,0:T(8,128)S(1)}, bf16[288,192]{1,0:T(8,128)(2,1)S(1)}, bf16[2,256,192]{2,1,0:T(8,128)(2,1)S(1)}...) custom-call(bf16[2,144,384]{2,1,0:T(8,128)(2,1)S(1)} %get-tuple-elem, ...), custom_call_target="tpu_custom_call" | custom-call | flops 1000000000 | tf_op jit(solution)/shard_map/pallas_call | solution.py:341
  13.6 0.0 collective-permute-done.1.refs_2_
  13.6 0.0 collective-permute-done.2.refs_3_
  13.7 0.0 copy-done.7
  13.7 0.0 copy-start.2
  13.7 1.8 %shard_map.125 = (f32[288,192]{1,0:T(8,128)S(1)}, f32[288,128]{1,0:T(8,128)S(1)}, bf16[288,192]{1,0:T(8,128)(2,1)S(1)}, bf16[2,256,192]{2,1,0:T(8,128)(2,1)S(1)}...) custom-call(bf16[2,144,384]{2,1,0:T(8,128)(2,1)S(1)} %get-tuple-elem, ...), custom_call_target="tpu_custom_call" | custom-call | flops 1000000000 | tf_op jit(solution)/shard_map/pallas_call | solution.py:341
  15.5 1.6 %collective-permute-start.6 = (bf16[2,144,256]{2,1,0:T(8,128)(2,1)S(1)}, bf16[2,144,256]{2,1,0:T(8,128)(2,1)S(1)}, u32[]{:S(2)}, u32[]{:S(2)}) collective-permute-start(bf16[2,144,256]{2,1,0:T(8,128)(2,1)S(1)} %get-tuple-element.59), channel_id=1, source_target_pairs={{0,1},{1,0},{2,3},{3,2},{4,5},{5,4},{6,7},{7,6},{8,9},{9,8},{10,11... | collective-permute-start | bytes 442376 | tf_op jit(solution)/shard_map/ppermute | solution.py:416
  17.0 0.5 %collective-permute-start.7 = (bf16[2,144,256]{2,1,0:T(8,128)(2,1)S(1)}, bf16[2,144,256]{2,1,0:T(8,128)(2,1)S(1)}, u32[]{:S(2)}, u32[]{:S(2)}) collective-permute-start(bf16[2,144,256]{2,1,0:T(8,128)(2,1)S(1)} %get-tuple-element.60), channel_id=1, source_target_pairs={{0,2},{1,3},{2,0},{3,1},{4,6},{5,7},{6,4},{7,5},{8,10},{9,11},{10,... | collective-permute-start | bytes 442376 | tf_op jit(solution)/shard_map/ppermute | solution.py:416
  17.5 1.5 %collective-permute-start.8 = (bf16[2,144,256]{2,1,0:T(8,128)(2,1)S(1)}, bf16[2,144,256]{2,1,0:T(8,128)(2,1)S(1)}, u32[]{:S(2)}, u32[]{:S(2)}) collective-permute-start(bf16[2,144,256]{2,1,0:T(8,128)(2,1)S(1)} %get-tuple-element.61), channel_id=1, source_target_pairs={{0,3},{1,2},{2,1},{3,0},{4,7},{5,6},{6,5},{7,4},{8,11},{9,10},{10,... | collective-permute-start | bytes 442376 | tf_op jit(solution)/shard_map/ppermute | solution.py:416
  19.0 0.0 copy-done.2
  19.0 0.0 copy-start.3
  19.0 1.7 %shard_map.126 = (bf16[2,144,192]{2,1,0:T(8,128)(2,1)S(1)}, bf16[2,144,192]{2,1,0:T(8,128)(2,1)S(1)}, bf16[2,48,192]{2,1,0:T(8,128)(2,1)S(1)}, bf16[2,48,192]{2,1,0:T(8,128)(2,1)S(1)}) custom-call(f32[288,192]{1,0:T(8,128)S(1)} %get-tuple-element.45.refs_0_, f32[288,128]{1,0:T(8,128)S(1)} %get-tuple-element.46.refs_1_, ...), custom_call_target="tpu_custom_call" | custom-call | tf_op jit(solution)/shard_map/pallas_call | solution.py:341
  20.7 0.0 copy-done.3
  20.7 1.7 %shard_map.127 = (bf16[2,144,192]{2,1,0:T(8,128)(2,1)S(1)}, bf16[144,384]{1,0:T(8,128)(2,1)S(1)}) custom-call(f32[288,192]{1,0:T(8,128)S(1)} %get-tuple-element.35.refs_0_, f32[288,128]{1,0:T(8,128)S(1)} %get-tuple-element.36.refs_1_, bf16[288,192]{1,0:T(8,128)(2,1)S(1)} %get-tuple-element.37.refs_2_, bf16[2,256,192]{2,1,0:T(8,128)(2,1)S(1)} %get-tuple-element.38.refs_3_, ...), custom_call_target="tpu_custom_call" | custom-call | tf_op jit(solution)/shard_map/pallas_call | solution.py:341
  22.4 0.1 collective-permute-start.3
  22.5 1.5 %collective-permute-start.4 = (bf16[2,48,192]{2,1,0:T(8,128)(2,1)S(1)}, bf16[2,48,192]{2,1,0:T(8,128)(2,1)S(1)}, u32[]{:S(2)}, u32[]{:S(2)}) collective-permute-start(bf16[2,48,192]{2,1,0:T(8,128)(2,1)S(1)} %get-tuple-element.56), channel_id=1, source_target_pairs={{0,1},{1,2},{2,3},{3,0},{4,5},{5,6},{6,7},{7,4},{8,9},{9,10},{10,1... | collective-permute-start | bytes 110600 | tf_op jit(solution)/shard_map/ppermute | solution.py:358
  24.0 0.0 collective-permute-done.6.refs_1_
  24.0 0.0 collective-permute-start.5
  24.0 2.4 %collective-permute-done.7.refs_2_ = bf16[2,144,256]{2,1,0:T(8,128)(2,1)S(1)} collective-permute-done((bf16[2,144,256]{2,1,0:T(8,128)(2,1)S(1)}, bf16[2,144,256]{2,1,0:T(8,128)(2,1)S(1)}, u32[]{:S(2)}, u32[]{:S(2)}) %collective-permute-start.7) | collective-permute-done | bytes 147488 | tf_op jit(solution)/shard_map/ppermute | solution.py:416
  26.5 0.0 collective-permute-done.8.refs_3_
  26.5 1.0 %shard_map.128 = (f32[432,1,144]{2,1,0:T(1,128)}, f32[8,128]{1,0:T(8,128)S(1)}) custom-call(bf16[2,144,256]{2,1,0:T(8,128)(2,1)S(1)} %get-tuple-element.58.refs_0_, bf16[2,144,256]{2,1,0:T(8,128)(2,1)S(1)} %collective-permute-done.6.refs_1_, bf16[2,144,256]{2,1,0:T(8,128)(2,1)S(1)} %collective-permute-done.7.refs_2_, ...), custom_call_target="tpu_custom_call" | custom-call | tf_op jit(solution)/shard_map/pallas_call | solution.py:341
  27.4 0.1 collective-permute-done.4.right
  27.5 3.6 %collective-permute-done.5.corner = bf16[2,48,192]{2,1,0:T(8,128)(2,1)S(1)} collective-permute-done((bf16[2,48,192]{2,1,0:T(8,128)(2,1)S(1)}, bf16[2,48,192]{2,1,0:T(8,128)(2,1)S(1)}, u32[]{:S(2)}, u32[]{:S(2)}) %collective-permute-start.5) | collective-permute-done | bytes 36896 | tf_op jit(solution)/shard_map/ppermute | solution.py:358
  31.2 0.0 collective-permute-done.3.below
  31.2 0.8 %shard_map.129 = bf16[4,6,24,192]{3,2,1,0:T(8,128)(2,1)} custom-call(bf16[2,144,192]{2,1,0:T(8,128)(2,1)S(1)} %get-tuple-element.54.inner, bf16[144,384]{1,0:T(8,128)(2,1)S(1)} %collective-permute-done.3.below, bf16[2,48,192]{2,1,0:T(8,128)(2,1)S(1)} %collective-permute-done.4.right, bf16[2,48,192]{2,1,0:T(8,128)(2,1)S(1)} %collective-permute-done.5.corner, ...), custom_call_target="tpu_custom_call" | custom-call | tf_op jit(solution)/shard_map/pallas_call | solution.py:341
Async XLA Ops:
  1.9 9.4 %collective-permute-start = (bf16[2,144,384]{2,1,0:T(8,128)(2,1)S(1)}, bf16[2,144,384]{2,1,0:T(8,128)(2,1)S(1)}, u32[]{:S(2)}, u32[]{:S(2)}) collective-permute-start(bf16[2,144,384]{2,1,0:T(8,128)(2,1)S(1)} %get-tuple-element.34), channel_id=1, source_target_pairs={{0,28},{1,29},{2,30},{3,31},{4,0},{5,1},{6,2},{7,3},{8,4},{9,5},{1... | collective-permute-start | bytes 663560 | tf_op jit(solution)/shard_map/ppermute | solution.py:358
  6.4 7.2 %collective-permute-start.1 = (bf16[2,48,384]{2,1,0:T(8,128)(2,1)S(1)}, bf16[2,48,384]{2,1,0:T(8,128)(2,1)S(1)}, u32[]{:S(2)}, u32[]{:S(2)}) collective-permute-start(bf16[2,48,384]{2,1,0:T(8,128)(2,1)S(1)} %get-tuple-element.42), channel_id=1, source_target_pairs={{0,3},{1,0},{2,1},{3,2},{4,7},{5,4},{6,5},{7,6},{8,11},{9,8},{10,9... | collective-permute-start | bytes 221192 | tf_op jit(solution)/shard_map/ppermute | solution.py:358
  8.9 4.8 %collective-permute-start.2 = (bf16[2,48,384]{2,1,0:T(8,128)(2,1)S(1)}, bf16[2,48,384]{2,1,0:T(8,128)(2,1)S(1)}, u32[]{:S(2)}, u32[]{:S(2)}) collective-permute-start(bf16[2,48,384]{2,1,0:T(8,128)(2,1)S(1)} %get-tuple-element.43), channel_id=1, source_target_pairs={{0,31},{1,28},{2,29},{3,30},{4,3},{5,0},{6,1},{7,2},{8,7},{9,4},{1... | collective-permute-start | bytes 221192 | tf_op jit(solution)/shard_map/ppermute | solution.py:358
  9.3 1.5 %copy-start.5 = (f32[2,1,6,144,144]{4,3,2,1,0:T(8,128)S(1)}, f32[2,1,6,144,144]{4,3,2,1,0:T(8,128)}, u32[]{:S(2)}) copy-start(f32[2,1,6,144,144]{4,3,2,1,0:T(8,128)} %param.16) | copy-start | bytes 2985988
  10.7 0.9 %copy-start = (bf16[192,576]{1,0:T(8,128)(2,1)S(1)}, bf16[192,576]{1,0:T(8,128)(2,1)}, u32[]{:S(2)}) copy-start(bf16[192,576]{1,0:T(8,128)(2,1)} %refs_8_.4) | copy-start | bytes 663556
  10.7 1.0 %copy-start.1 = (bf16[4,64,144]{2,1,0:T(8,128)(2,1)S(1)}, bf16[4,64,144]{2,1,0:T(8,128)(2,1)}, u32[]{:S(2)}) copy-start(bf16[4,64,144]{2,1,0:T(8,128)(2,1)} %constant.10.clone.refs_7_.refs_9_.refs_10_) | copy-start | bytes 221188
  10.7 1.0 %copy-start.4 = (f32[192]{0:T(256)S(1)}, f32[192]{0:T(256)}, u32[]{:S(2)}) copy-start(f32[192]{0:T(256)} %param.13) | copy-start | bytes 2308
  10.7 1.1 %copy-start.6 = (bf16[192,192]{1,0:T(8,128)(2,1)S(1)}, bf16[192,192]{1,0:T(8,128)(2,1)}, u32[]{:S(2)}) copy-start(bf16[192,192]{1,0:T(8,128)(2,1)} %refs_6_.2) | copy-start | bytes 221188
  10.7 1.1 %copy-start.8 = (bf16[144,288]{1,0:T(8,128)(2,1)S(1)}, bf16[144,288]{1,0:T(8,128)(2,1)}, u32[]{:S(2)}) copy-start(bf16[144,288]{1,0:T(8,128)(2,1)} %constant.11.clone.refs_6_) | copy-start | bytes 248836
  11.9 1.8 %copy-start.7 = (bf16[144,384]{1,0:T(8,128)(2,1)S(1)}, bf16[144,384]{1,0:T(8,128)(2,1)}, u32[]{:S(2)}) copy-start(bf16[144,384]{1,0:T(8,128)(2,1)} %constant.12.clone.refs_8_) | copy-start | bytes 331780
  13.7 5.3 %copy-start.2 = (bf16[384,144]{1,0:T(8,128)(2,1)S(1)}, bf16[384,144]{1,0:T(8,128)(2,1)}, u32[]{:S(2)}) copy-start(bf16[384,144]{1,0:T(8,128)(2,1)} %constant.13.clone.refs_9_) | copy-start | bytes 331780
  15.5 8.6 %collective-permute-start.6 = (bf16[2,144,256]{2,1,0:T(8,128)(2,1)S(1)}, bf16[2,144,256]{2,1,0:T(8,128)(2,1)S(1)}, u32[]{:S(2)}, u32[]{:S(2)}) collective-permute-start(bf16[2,144,256]{2,1,0:T(8,128)(2,1)S(1)} %get-tuple-element.59), channel_id=1, source_target_pairs={{0,1},{1,0},{2,3},{3,2},{4,5},{5,4},{6,7},{7,6},{8,9},{9,8},{10,11... | collective-permute-start | bytes 442376 | tf_op jit(solution)/shard_map/ppermute | solution.py:416
  17.0 9.4 %collective-permute-start.7 = (bf16[2,144,256]{2,1,0:T(8,128)(2,1)S(1)}, bf16[2,144,256]{2,1,0:T(8,128)(2,1)S(1)}, u32[]{:S(2)}, u32[]{:S(2)}) collective-permute-start(bf16[2,144,256]{2,1,0:T(8,128)(2,1)S(1)} %get-tuple-element.60), channel_id=1, source_target_pairs={{0,2},{1,3},{2,0},{3,1},{4,6},{5,7},{6,4},{7,5},{8,10},{9,11},{10,... | collective-permute-start | bytes 442376 | tf_op jit(solution)/shard_map/ppermute | solution.py:416
  17.5 8.9 %collective-permute-start.8 = (bf16[2,144,256]{2,1,0:T(8,128)(2,1)S(1)}, bf16[2,144,256]{2,1,0:T(8,128)(2,1)S(1)}, u32[]{:S(2)}, u32[]{:S(2)}) collective-permute-start(bf16[2,144,256]{2,1,0:T(8,128)(2,1)S(1)} %get-tuple-element.61), channel_id=1, source_target_pairs={{0,3},{1,2},{2,1},{3,0},{4,7},{5,6},{6,5},{7,4},{8,11},{9,10},{10,... | collective-permute-start | bytes 442376 | tf_op jit(solution)/shard_map/ppermute | solution.py:416
  19.0 1.7 %copy-start.3 = (bf16[288,144]{1,0:T(8,128)(2,1)S(1)}, bf16[288,144]{1,0:T(8,128)(2,1)}, u32[]{:S(2)}) copy-start(bf16[288,144]{1,0:T(8,128)(2,1)} %constant.14.clone.refs_9_) | copy-start | bytes 248836
  22.4 8.7 %collective-permute-start.3 = (bf16[144,384]{1,0:T(8,128)(2,1)S(1)}, bf16[144,384]{1,0:T(8,128)(2,1)S(1)}, u32[]{:S(2)}, u32[]{:S(2)}) collective-permute-start(bf16[144,384]{1,0:T(8,128)(2,1)S(1)} %get-tuple-element.55), channel_id=1, source_target_pairs={{0,4},{1,5},{2,6},{3,7},{4,8},{5,9},{6,10},{7,11},{8,12},{9,13},{1... | collective-permute-start | bytes 331784 | tf_op jit(solution)/shard_map/ppermute | solution.py:358
  22.5 5.0 %collective-permute-start.4 = (bf16[2,48,192]{2,1,0:T(8,128)(2,1)S(1)}, bf16[2,48,192]{2,1,0:T(8,128)(2,1)S(1)}, u32[]{:S(2)}, u32[]{:S(2)}) collective-permute-start(bf16[2,48,192]{2,1,0:T(8,128)(2,1)S(1)} %get-tuple-element.56), channel_id=1, source_target_pairs={{0,1},{1,2},{2,3},{3,0},{4,5},{5,6},{6,7},{7,4},{8,9},{9,10},{10,1... | collective-permute-start | bytes 110600 | tf_op jit(solution)/shard_map/ppermute | solution.py:358
  24.0 7.1 %collective-permute-start.5 = (bf16[2,48,192]{2,1,0:T(8,128)(2,1)S(1)}, bf16[2,48,192]{2,1,0:T(8,128)(2,1)S(1)}, u32[]{:S(2)}, u32[]{:S(2)}) collective-permute-start(bf16[2,48,192]{2,1,0:T(8,128)(2,1)S(1)} %get-tuple-element.57), channel_id=1, source_target_pairs={{0,5},{1,6},{2,7},{3,4},{4,9},{5,10},{6,11},{7,8},{8,13},{9,14},{1... | collective-permute-start | bytes 110600 | tf_op jit(solution)/shard_map/ppermute | solution.py:358

commit v4 on v3

--- a/solution.py
+++ b/solution.py
@@ -85,17 +85,26 @@
     return table
 
 
-def send_kernel(both, inner, below, right, corner):
+def send_kernel(both, inner, below):
     levels = both.shape[0]
     for a in range(levels // WZ):
         at = [(a * WZ + WZ // 2 + z) % levels for z in range(WZ)]
-        for whole, side, base in ((below, corner, 0), (inner, right, HALF_ROWS)):
+        for whole, base in ((below, 0), (inner, HALF_ROWS)):
             rows = [both[level, base + row].astype(F32) for level in at for row in range(HALF_ROWS)]
             whole[a] = jnp.concatenate(rows, axis=0).astype(BF16)
-            side[a] = jnp.concatenate([row[:SIDE] for row in rows], axis=0).astype(BF16)
-
-
-def prep_kernel(chunks, lat_count, bias, bias_t):
+
+
+def side_kernel(both, after, right, corner):
+    levels = both.shape[0]
+    for a in range(levels // WZ):
+        at = [(a * WZ + WZ // 2 + z) % levels for z in range(WZ)]
+        for side, base in ((corner, 0), (right, HALF_ROWS)):
+            rows = [both[level, base + row].astype(F32)[:SIDE] for level in at for row in range(HALF_ROWS)]
+            side[a] = jnp.concatenate(rows, axis=0).astype(BF16)
+
+
+def prep_kernel(chunks, lat_count, bias, bias_t, after):
+    after[...] = jnp.zeros(after.shape, F32)
     level_windows = bias.shape[0]
     last_lat = lax.axis_index("lat") == lat_count - 1
     me = lax.axis_index("lon")
@@ -369,20 +378,24 @@
     gain = norm_gain.reshape(1, channels)
     queries = jnp.asarray(chunks.queries(), BF16)
 
-    inner, below, right, corner = call(
-        send_kernel,
-        [struct((level_windows, size, 2 * channels), BF16) for size in (half, half, side, side)],
-        (jnp.concatenate([tokens, cotangent], axis=-1),),
+    both = jnp.concatenate([tokens, cotangent], axis=-1)
+    inner, below = call(
+        send_kernel, [struct((level_windows, half, 2 * channels), BF16)] * 2, (both,)
     )
     below = shift(below, -1, 0)
+    bias_t, after = call(
+        functools.partial(prep_kernel, chunks, lat_count),
+        [
+            struct((level_windows, lon_count, WT, chunks.width), F32),
+            struct((8, LANES), F32),
+        ],
+        (bias.reshape(level_windows, heads, WT, WT),),
+    )
+    right, corner = call(
+        side_kernel, [struct((level_windows, side, 2 * channels), BF16)] * 2, (both, after)
+    )
     right = shift(right, 0, -1)
     corner = shift(corner, -1, -1)
-    (bias_t,) = call(
-        functools.partial(prep_kernel, chunks, lat_count),
-        [struct((level_windows, lon_count, WT, chunks.width), F32)],
-        (bias.reshape(level_windows, heads, WT, WT),),
-        flops=10**9,
-    )
     per_window = []
     total = []
     for c in range(windows):
@@ -427,7 +440,8 @@
         )
         grads = results[:2]
         if last:
-            left, corner = shift(results[2], 0, 1), shift(results[3], 1, 1)
+            corner = shift(results[3], 1, 1)
+            left = shift(results[2], 0, 1)
     above = shift(grads[1], 1, 0)
     bias_grad, after = call(
         functools.partial(bias_kernel, chunks),

time: 32.1 us -> 33.1 us (1.031)
  waiting for transfers between devices: 6.12 us -> 7.64 us
  local copies, waits for them, and re-layouts: 2.04 us -> 1.52 us
    ppermute x6, waiting for transfers between devices: 3.71 us -> 7.11 us  [shift(): return lax.ppermute(value, ('lat', 'lon'), pairs)]
    ppermute x3, waiting for transfers between devices: 2.41 us -> 0.53 us  [local(): arrived.append(lax.ppermute(total[d], 'lon', pairs))]
    unnamed x18, local copies, waits for them, and re-layouts: 2.04 us -> 1.52 us
    pallas_call x8 -> x9, Pallas kernels: 9.33 us -> 9.33 us  [call(): pl.pallas_call(kernel, out_shape=outs, in_specs=vmem(len(args)), out_spec...]
  transfers between devices with their start and end apart: 9 -> 9, of which waited for: 3 -> 5; matrix products, arithmetic and copies ran while one was open for 0% -> 0% of each run, Pallas kernels for 21% -> 20%
where the time goes in v4:
time: 33.1 us; the launch traced here: 33 us
  starting transfers between devices  12.4 us (37%)
  Pallas kernels  9.33 us (28%)
  waiting for transfers between devices  7.64 us (23%)
  local copies, waits for them, and re-layouts  1.52 us (5%)
  other arithmetic  1.25 us (4%)
  between operations  0.78 us (2%)
    pallas_call x9, Pallas kernels, call(): pl.pallas_call(kernel, out_shape=outs, in_specs=vmem(len(args)), out_spec...  9.33 us
    ppermute x6, starting transfers between devices, shift(): return lax.ppermute(value, ('lat', 'lon'), pairs)  8.89 us
    ppermute x6, waiting for transfers between devices, shift(): return lax.ppermute(value, ('lat', 'lon'), pairs)  7.11 us
    ppermute x3, starting transfers between devices, local(): arrived.append(lax.ppermute(total[d], 'lon', pairs))  3.55 us
    unnamed x18, local copies, waits for them, and re-layouts  1.52 us
    concatenate x1, other arithmetic, local(): both = jnp.concatenate([tokens, cotangent], axis=-1)  1.25 us
  transfers between devices with their start and end apart: 9, of which 5 were waited for; matrix products, arithmetic and copies ran while one was open for 0% of the time, Pallas kernels for 20%

profile of v4, /device:TPU:0, one launch (start us, length us, event | category | flops | bytes accessed | tf_op | source)
XLA Modules:
  0.0 33.0 jit_solution(14743257610444200688)
XLA Ops:
  0.6 0.0 copy-start.6
  0.6 0.0 copy-start.8
  0.7 1.2 %pad_maximum_fusion.both = bf16[4,6,24,384]{3,2,1,0:T(8,128)(2,1)S(1)} fusion(bf16[4,6,24,192]{3,2,1,0:T(8,128)(2,1)} %param.12, bf16[4,6,24,192]{3,2,1,0:T(8,128)(2,1)} %param.11), kind=kLoop, calls=%fused_computation | loop fusion | flops 884736 | bytes 884736 | tf_op jit(solution)/shard_map/concatenate | solution.py:381
  1.9 0.0 copy-start.1
  1.9 0.0 copy-start.2
  2.0 0.0 copy-start.5
  2.0 4.5 %collective-permute-start = (bf16[2,144,384]{2,1,0:T(8,128)(2,1)S(1)}, bf16[2,144,384]{2,1,0:T(8,128)(2,1)S(1)}, u32[]{:S(2)}, u32[]{:S(2)}) collective-permute-start(bf16[2,144,384]{2,1,0:T(8,128)(2,1)S(1)} %get-tuple-element.36), channel_id=1, source_target_pairs={{0,28},{1,29},{2,30},{3,31},{4,0},{5,1},{6,2},{7,3},{8,4},{9,5},{1... | collective-permute-start | bytes 663560 | tf_op jit(solution)/shard_map/ppermute | solution.py:367
  6.5 0.0 copy-start
  6.5 1.5 %copy-done = f32[2,1,6,144,144]{4,3,2,1,0:T(8,128)S(1)} copy-done((f32[2,1,6,144,144]{4,3,2,1,0:T(8,128)S(1)}, f32[2,1,6,144,144]{4,3,2,1,0:T(8,128)}, u32[]{:S(2)}) %copy-start) | copy-done | bytes 995352
  8.0 0.6 %shard_map.123 = (f32[2,4,144,256]{3,2,1,0:T(8,128)S(1)}, f32[8,128]{1,0:T(8,128)S(1)}) custom-call(f32[2,6,144,144]{3,2,1,0:T(8,128)S(1)} %bitcast.3), custom_call_target="tpu_custom_call" | custom-call | tf_op jit(solution)/shard_map/pallas_call | solution.py:350
  8.6 2.5 %collective-permute-start.1 = (bf16[2,48,384]{2,1,0:T(8,128)(2,1)S(1)}, bf16[2,48,384]{2,1,0:T(8,128)(2,1)S(1)}, u32[]{:S(2)}, u32[]{:S(2)}) collective-permute-start(bf16[2,48,384]{2,1,0:T(8,128)(2,1)S(1)} %get-tuple-element.46), channel_id=1, source_target_pairs={{0,3},{1,0},{2,1},{3,2},{4,7},{5,4},{6,5},{7,6},{8,11},{9,8},{10,9... | collective-permute-start | bytes 221192 | tf_op jit(solution)/shard_map/ppermute | solution.py:367
  11.1 0.4 %collective-permute-start.2 = (bf16[2,48,384]{2,1,0:T(8,128)(2,1)S(1)}, bf16[2,48,384]{2,1,0:T(8,128)(2,1)S(1)}, u32[]{:S(2)}, u32[]{:S(2)}) collective-permute-start(bf16[2,48,384]{2,1,0:T(8,128)(2,1)S(1)} %get-tuple-element.47), channel_id=1, source_target_pairs={{0,31},{1,28},{2,29},{3,30},{4,3},{5,0},{6,1},{7,2},{8,7},{9,4},{1... | collective-permute-start | bytes 221192 | tf_op jit(solution)/shard_map/ppermute | solution.py:367
  11.5 0.0 collective-permute-done.refs_1_
  11.5 0.0 copy-done.6
  11.5 0.0 copy-done.8
  11.5 0.0 copy-done.1
  11.5 0.0 copy-done.2
  11.5 0.0 copy-done.5
  11.5 0.0 copy-start.7
  11.5 1.7 %shard_map.124 = (f32[288,192]{1,0:T(8,128)S(1)}, f32[288,128]{1,0:T(8,128)S(1)}, bf16[288,192]{1,0:T(8,128)(2,1)S(1)}, bf16[2,256,192]{2,1,0:T(8,128)(2,1)S(1)}...) custom-call(bf16[2,144,384]{2,1,0:T(8,128)(2,1)S(1)} %get-tuple-elem, ...), custom_call_target="tpu_custom_call" | custom-call | flops 1000000000 | tf_op jit(solution)/shard_map/pallas_call | solution.py:350
  13.3 0.5 %collective-permute-done.1.refs_2_ = bf16[2,48,384]{2,1,0:T(8,128)(2,1)S(1)} collective-permute-done((bf16[2,48,384]{2,1,0:T(8,128)(2,1)S(1)}, bf16[2,48,384]{2,1,0:T(8,128)(2,1)S(1)}, u32[]{:S(2)}, u32[]{:S(2)}) %collective-permute-start.1) | collective-permute-done | bytes 73760 | tf_op jit(solution)/shard_map/ppermute | solution.py:367
  13.8 1.1 %collective-permute-done.2.refs_3_ = bf16[2,48,384]{2,1,0:T(8,128)(2,1)S(1)} collective-permute-done((bf16[2,48,384]{2,1,0:T(8,128)(2,1)S(1)}, bf16[2,48,384]{2,1,0:T(8,128)(2,1)S(1)}, u32[]{:S(2)}, u32[]{:S(2)}) %collective-permute-start.2) | collective-permute-done | bytes 73760 | tf_op jit(solution)/shard_map/ppermute | solution.py:367
  14.9 0.0 copy-done.7
  14.9 0.0 copy-start.3
  14.9 1.8 %shard_map.126 = (f32[288,192]{1,0:T(8,128)S(1)}, f32[288,128]{1,0:T(8,128)S(1)}, bf16[288,192]{1,0:T(8,128)(2,1)S(1)}, bf16[2,256,192]{2,1,0:T(8,128)(2,1)S(1)}...) custom-call(bf16[2,144,384]{2,1,0:T(8,128)(2,1)S(1)} %get-tuple-elem, ...), custom_call_target="tpu_custom_call" | custom-call | flops 1000000000 | tf_op jit(solution)/shard_map/pallas_call | solution.py:350
  16.7 1.3 %collective-permute-start.6 = (bf16[2,144,256]{2,1,0:T(8,128)(2,1)S(1)}, bf16[2,144,256]{2,1,0:T(8,128)(2,1)S(1)}, u32[]{:S(2)}, u32[]{:S(2)}) collective-permute-start(bf16[2,144,256]{2,1,0:T(8,128)(2,1)S(1)} %get-tuple-element.63), channel_id=1, source_target_pairs={{0,1},{1,0},{2,3},{3,2},{4,5},{5,4},{6,7},{7,6},{8,9},{9,8},{10,11... | collective-permute-start | bytes 442376 | tf_op jit(solution)/shard_map/ppermute | solution.py:429
  18.0 1.5 %collective-permute-start.7 = (bf16[2,144,256]{2,1,0:T(8,128)(2,1)S(1)}, bf16[2,144,256]{2,1,0:T(8,128)(2,1)S(1)}, u32[]{:S(2)}, u32[]{:S(2)}) collective-permute-start(bf16[2,144,256]{2,1,0:T(8,128)(2,1)S(1)} %get-tuple-element.64), channel_id=1, source_target_pairs={{0,2},{1,3},{2,0},{3,1},{4,6},{5,7},{6,4},{7,5},{8,10},{9,11},{10,... | collective-permute-start | bytes 442376 | tf_op jit(solution)/shard_map/ppermute | solution.py:429
  19.5 0.7 %collective-permute-start.8 = (bf16[2,144,256]{2,1,0:T(8,128)(2,1)S(1)}, bf16[2,144,256]{2,1,0:T(8,128)(2,1)S(1)}, u32[]{:S(2)}, u32[]{:S(2)}) collective-permute-start(bf16[2,144,256]{2,1,0:T(8,128)(2,1)S(1)} %get-tuple-element.65), channel_id=1, source_target_pairs={{0,3},{1,2},{2,1},{3,0},{4,7},{5,6},{6,5},{7,4},{8,11},{9,10},{10,... | collective-permute-start | bytes 442376 | tf_op jit(solution)/shard_map/ppermute | solution.py:429
  20.2 0.0 copy-done.3
  20.2 0.0 copy-start.4
  20.2 1.7 %shard_map.127 = (bf16[2,144,192]{2,1,0:T(8,128)(2,1)S(1)}, bf16[2,144,192]{2,1,0:T(8,128)(2,1)S(1)}, bf16[2,48,192]{2,1,0:T(8,128)(2,1)S(1)}, bf16[2,48,192]{2,1,0:T(8,128)(2,1)S(1)}) custom-call(f32[288,192]{1,0:T(8,128)S(1)} %get-tuple-element.49.refs_0_, f32[288,128]{1,0:T(8,128)S(1)} %get-tuple-element.50.refs_1_, ...), custom_call_target="tpu_custom_call" | custom-call | tf_op jit(solution)/shard_map/pallas_call | solution.py:350
  21.9 0.0 copy-done.4
  21.9 1.7 %shard_map.128 = (bf16[2,144,192]{2,1,0:T(8,128)(2,1)S(1)}, bf16[144,384]{1,0:T(8,128)(2,1)S(1)}) custom-call(f32[288,192]{1,0:T(8,128)S(1)} %get-tuple-element.38.refs_0_, f32[288,128]{1,0:T(8,128)S(1)} %get-tuple-element.39.refs_1_, bf16[288,192]{1,0:T(8,128)(2,1)S(1)} %get-tuple-element.40.refs_2_, bf16[2,256,192]{2,1,0:T(8,128)(2,1)S(1)} %get-tuple-element.41.refs_3_, ...), custom_call_target="tpu_custom_call" | custom-call | tf_op jit(solution)/shard_map/pallas_call | solution.py:350
  23.6 0.1 collective-permute-start.3
  23.7 1.3 %collective-permute-start.4 = (bf16[2,48,192]{2,1,0:T(8,128)(2,1)S(1)}, bf16[2,48,192]{2,1,0:T(8,128)(2,1)S(1)}, u32[]{:S(2)}, u32[]{:S(2)}) collective-permute-start(bf16[2,48,192]{2,1,0:T(8,128)(2,1)S(1)} %get-tuple-element.60), channel_id=1, source_target_pairs={{0,1},{1,2},{2,3},{3,0},{4,5},{5,6},{6,7},{7,4},{8,9},{9,10},{10,1... | collective-permute-start | bytes 110600 | tf_op jit(solution)/shard_map/ppermute | solution.py:367
  25.0 0.0 collective-permute-done.6.refs_1_
  25.0 0.1 collective-permute-start.5
  25.1 0.0 collective-permute-done.7.refs_2_
  25.1 0.5 %collective-permute-done.8.refs_3_ = bf16[2,144,256]{2,1,0:T(8,128)(2,1)S(1)} collective-permute-done((bf16[2,144,256]{2,1,0:T(8,128)(2,1)S(1)}, bf16[2,144,256]{2,1,0:T(8,128)(2,1)S(1)}, u32[]{:S(2)}, u32[]{:S(2)}) %collective-permute-start.8) | collective-permute-done | bytes 147488 | tf_op jit(solution)/shard_map/ppermute | solution.py:429
  25.7 1.0 %shard_map.129 = (f32[432,1,144]{2,1,0:T(1,128)}, f32[8,128]{1,0:T(8,128)S(1)}) custom-call(bf16[2,144,256]{2,1,0:T(8,128)(2,1)S(1)} %get-tuple-element.62.refs_0_, bf16[2,144,256]{2,1,0:T(8,128)(2,1)S(1)} %collective-permute-done.6.refs_1_, bf16[2,144,256]{2,1,0:T(8,128)(2,1)S(1)} %collective-permute-done.7.refs_2_, ...), custom_call_target="tpu_custom_call" | custom-call | tf_op jit(solution)/shard_map/pallas_call | solution.py:350
  26.6 2.1 %collective-permute-done.4.right = bf16[2,48,192]{2,1,0:T(8,128)(2,1)S(1)} collective-permute-done((bf16[2,48,192]{2,1,0:T(8,128)(2,1)S(1)}, bf16[2,48,192]{2,1,0:T(8,128)(2,1)S(1)}, u32[]{:S(2)}, u32[]{:S(2)}) %collective-permute-start.4) | collective-permute-done | bytes 36896 | tf_op jit(solution)/shard_map/ppermute | solution.py:367
  28.7 3.4 %collective-permute-done.5.corner = bf16[2,48,192]{2,1,0:T(8,128)(2,1)S(1)} collective-permute-done((bf16[2,48,192]{2,1,0:T(8,128)(2,1)S(1)}, bf16[2,48,192]{2,1,0:T(8,128)(2,1)S(1)}, u32[]{:S(2)}, u32[]{:S(2)}) %collective-permute-start.5) | collective-permute-done | bytes 36896 | tf_op jit(solution)/shard_map/ppermute | solution.py:367
  32.2 0.0 collective-permute-done.3.below
  32.2 0.8 %shard_map.130 = bf16[4,6,24,192]{3,2,1,0:T(8,128)(2,1)} custom-call(bf16[2,144,192]{2,1,0:T(8,128)(2,1)S(1)} %get-tuple-element.58.inner, bf16[144,384]{1,0:T(8,128)(2,1)S(1)} %collective-permute-done.3.below, bf16[2,48,192]{2,1,0:T(8,128)(2,1)S(1)} %collective-permute-done.4.right, bf16[2,48,192]{2,1,0:T(8,128)(2,1)S(1)} %collective-permute-done.5.corner, ...), custom_call_target="tpu_custom_call" | custom-call | tf_op jit(solution)/shard_map/pallas_call | solution.py:350
  (2 shorter events, 0.1 us)
Async XLA Ops:
  0.6 10.8 %copy-start.6 = (bf16[192,192]{1,0:T(8,128)(2,1)S(1)}, bf16[192,192]{1,0:T(8,128)(2,1)}, u32[]{:S(2)}) copy-start(bf16[192,192]{1,0:T(8,128)(2,1)} %refs_6_.2) | copy-start | bytes 221188
  0.6 10.8 %copy-start.8 = (bf16[144,288]{1,0:T(8,128)(2,1)S(1)}, bf16[144,288]{1,0:T(8,128)(2,1)}, u32[]{:S(2)}) copy-start(bf16[144,288]{1,0:T(8,128)(2,1)} %constant.11.clone.refs_6_) | copy-start | bytes 248836
  1.9 9.6 %copy-start.1 = (bf16[192,576]{1,0:T(8,128)(2,1)S(1)}, bf16[192,576]{1,0:T(8,128)(2,1)}, u32[]{:S(2)}) copy-start(bf16[192,576]{1,0:T(8,128)(2,1)} %refs_8_.4) | copy-start | bytes 663556
  1.9 9.6 %copy-start.2 = (bf16[4,64,144]{2,1,0:T(8,128)(2,1)S(1)}, bf16[4,64,144]{2,1,0:T(8,128)(2,1)}, u32[]{:S(2)}) copy-start(bf16[4,64,144]{2,1,0:T(8,128)(2,1)} %constant.10.clone.refs_7_.refs_9_.refs_10_) | copy-start | bytes 221188
  2.0 9.5 %copy-start.5 = (f32[192]{0:T(256)S(1)}, f32[192]{0:T(256)}, u32[]{:S(2)}) copy-start(f32[192]{0:T(256)} %param.13) | copy-start | bytes 2308
  2.0 9.5 %collective-permute-start = (bf16[2,144,384]{2,1,0:T(8,128)(2,1)S(1)}, bf16[2,144,384]{2,1,0:T(8,128)(2,1)S(1)}, u32[]{:S(2)}, u32[]{:S(2)}) collective-permute-start(bf16[2,144,384]{2,1,0:T(8,128)(2,1)S(1)} %get-tuple-element.36), channel_id=1, source_target_pairs={{0,28},{1,29},{2,30},{3,31},{4,0},{5,1},{6,2},{7,3},{8,4},{9,5},{1... | collective-permute-start | bytes 663560 | tf_op jit(solution)/shard_map/ppermute | solution.py:367
  6.5 1.5 %copy-start = (f32[2,1,6,144,144]{4,3,2,1,0:T(8,128)S(1)}, f32[2,1,6,144,144]{4,3,2,1,0:T(8,128)}, u32[]{:S(2)}) copy-start(f32[2,1,6,144,144]{4,3,2,1,0:T(8,128)} %param.16) | copy-start | bytes 2985988
  8.6 5.2 %collective-permute-start.1 = (bf16[2,48,384]{2,1,0:T(8,128)(2,1)S(1)}, bf16[2,48,384]{2,1,0:T(8,128)(2,1)S(1)}, u32[]{:S(2)}, u32[]{:S(2)}) collective-permute-start(bf16[2,48,384]{2,1,0:T(8,128)(2,1)S(1)} %get-tuple-element.46), channel_id=1, source_target_pairs={{0,3},{1,0},{2,1},{3,2},{4,7},{5,4},{6,5},{7,6},{8,11},{9,8},{10,9... | collective-permute-start | bytes 221192 | tf_op jit(solution)/shard_map/ppermute | solution.py:367
  11.1 3.8 %collective-permute-start.2 = (bf16[2,48,384]{2,1,0:T(8,128)(2,1)S(1)}, bf16[2,48,384]{2,1,0:T(8,128)(2,1)S(1)}, u32[]{:S(2)}, u32[]{:S(2)}) collective-permute-start(bf16[2,48,384]{2,1,0:T(8,128)(2,1)S(1)} %get-tuple-element.47), channel_id=1, source_target_pairs={{0,31},{1,28},{2,29},{3,30},{4,3},{5,0},{6,1},{7,2},{8,7},{9,4},{1... | collective-permute-start | bytes 221192 | tf_op jit(solution)/shard_map/ppermute | solution.py:367
  11.5 3.4 %copy-start.7 = (bf16[144,384]{1,0:T(8,128)(2,1)S(1)}, bf16[144,384]{1,0:T(8,128)(2,1)}, u32[]{:S(2)}) copy-start(bf16[144,384]{1,0:T(8,128)(2,1)} %constant.12.clone.refs_8_) | copy-start | bytes 331780
  14.9 5.3 %copy-start.3 = (bf16[384,144]{1,0:T(8,128)(2,1)S(1)}, bf16[384,144]{1,0:T(8,128)(2,1)}, u32[]{:S(2)}) copy-start(bf16[384,144]{1,0:T(8,128)(2,1)} %constant.13.clone.refs_9_) | copy-start | bytes 331780
  16.7 8.4 %collective-permute-start.6 = (bf16[2,144,256]{2,1,0:T(8,128)(2,1)S(1)}, bf16[2,144,256]{2,1,0:T(8,128)(2,1)S(1)}, u32[]{:S(2)}, u32[]{:S(2)}) collective-permute-start(bf16[2,144,256]{2,1,0:T(8,128)(2,1)S(1)} %get-tuple-element.63), channel_id=1, source_target_pairs={{0,1},{1,0},{2,3},{3,2},{4,5},{5,4},{6,7},{7,6},{8,9},{9,8},{10,11... | collective-permute-start | bytes 442376 | tf_op jit(solution)/shard_map/ppermute | solution.py:429
  18.0 7.1 %collective-permute-start.7 = (bf16[2,144,256]{2,1,0:T(8,128)(2,1)S(1)}, bf16[2,144,256]{2,1,0:T(8,128)(2,1)S(1)}, u32[]{:S(2)}, u32[]{:S(2)}) collective-permute-start(bf16[2,144,256]{2,1,0:T(8,128)(2,1)S(1)} %get-tuple-element.64), channel_id=1, source_target_pairs={{0,2},{1,3},{2,0},{3,1},{4,6},{5,7},{6,4},{7,5},{8,10},{9,11},{10,... | collective-permute-start | bytes 442376 | tf_op jit(solution)/shard_map/ppermute | solution.py:429
  19.5 6.1 %collective-permute-start.8 = (bf16[2,144,256]{2,1,0:T(8,128)(2,1)S(1)}, bf16[2,144,256]{2,1,0:T(8,128)(2,1)S(1)}, u32[]{:S(2)}, u32[]{:S(2)}) collective-permute-start(bf16[2,144,256]{2,1,0:T(8,128)(2,1)S(1)} %get-tuple-element.65), channel_id=1, source_target_pairs={{0,3},{1,2},{2,1},{3,0},{4,7},{5,6},{6,5},{7,4},{8,11},{9,10},{10,... | collective-permute-start | bytes 442376 | tf_op jit(solution)/shard_map/ppermute | solution.py:429
  20.2 1.7 %copy-start.4 = (bf16[288,144]{1,0:T(8,128)(2,1)S(1)}, bf16[288,144]{1,0:T(8,128)(2,1)}, u32[]{:S(2)}) copy-start(bf16[288,144]{1,0:T(8,128)(2,1)} %constant.14.clone.refs_9_) | copy-start | bytes 248836
  23.6 8.5 %collective-permute-start.3 = (bf16[144,384]{1,0:T(8,128)(2,1)S(1)}, bf16[144,384]{1,0:T(8,128)(2,1)S(1)}, u32[]{:S(2)}, u32[]{:S(2)}) collective-permute-start(bf16[144,384]{1,0:T(8,128)(2,1)S(1)} %get-tuple-element.59), channel_id=1, source_target_pairs={{0,4},{1,5},{2,6},{3,7},{4,8},{5,9},{6,10},{7,11},{8,12},{9,13},{1... | collective-permute-start | bytes 331784 | tf_op jit(solution)/shard_map/ppermute | solution.py:367
  23.7 5.0 %collective-permute-start.4 = (bf16[2,48,192]{2,1,0:T(8,128)(2,1)S(1)}, bf16[2,48,192]{2,1,0:T(8,128)(2,1)S(1)}, u32[]{:S(2)}, u32[]{:S(2)}) collective-permute-start(bf16[2,48,192]{2,1,0:T(8,128)(2,1)S(1)} %get-tuple-element.60), channel_id=1, source_target_pairs={{0,1},{1,2},{2,3},{3,0},{4,5},{5,6},{6,7},{7,4},{8,9},{9,10},{10,1... | collective-permute-start | bytes 110600 | tf_op jit(solution)/shard_map/ppermute | solution.py:367
  25.0 7.1 %collective-permute-start.5 = (bf16[2,48,192]{2,1,0:T(8,128)(2,1)S(1)}, bf16[2,48,192]{2,1,0:T(8,128)(2,1)S(1)}, u32[]{:S(2)}, u32[]{:S(2)}) collective-permute-start(bf16[2,48,192]{2,1,0:T(8,128)(2,1)S(1)} %get-tuple-element.61), channel_id=1, source_target_pairs={{0,5},{1,6},{2,7},{3,4},{4,9},{5,10},{6,11},{7,8},{8,13},{9,14},{1... | collective-permute-start | bytes 110600 | tf_op jit(solution)/shard_map/ppermute | solution.py:367
